TPU v7x, 32 devices: a whole 2x2x4 slice. The times are simulated.
32 devices in a mesh: panel: 2 (over core), lon: 8 (over z, x), lat: 2 (over y).
Axes of the slice: x: 2, y: 2, z: 4, core: 2. Of those that a mesh axis runs over, the one named last changes fastest.
Arguments:
- fields: float32 [2, 24, 256, 256], P('panel', None, 'lon', 'lat'), may hold values from -6 to 6
- offsets: int32 [2, 2, 32, 2], P('panel', None, 'lon', 'lat'), may hold values from -7 to 7
- fractions: float32 [2, 2, 256, 256], P('panel', None, 'lon', 'lat'), may hold values from 0 to 1
- send_count: int32 [2, 8, 2], P('panel', 'lon', 'lat'), may hold values from 0 to 64, as said below
- send_owner: int32 [2, 8, 2, 64], P('panel', 'lon', 'lat'), may hold values from 0 to 7, as said below
- send_cell: int32 [2, 8, 2, 64], P('panel', 'lon', 'lat'), may hold values from 0 to 3966, as said below
- send_target: int32 [2, 8, 2, 64], P('panel', 'lon', 'lat'), may hold values from 0 to 127, as said below
- send_frac: float32 [2, 8, 2, 2, 64], P('panel', 'lon', 'lat'), may hold values from 0 to 1
Outputs:
- advected_fields: float32 [2, 24, 256, 256], P('panel', None, 'lon', 'lat')
Inputs may be any that keep to these rules, and one draw needn't show every extreme that they name: `send_count`: 64 on the devices that give donor values and 0 elsewhere; in each row of devices along longitude (one panel, one latitude index) the donors are the first 4 or the last 4 longitude indices. `send_owner`: the receiving device lies on the other panel at the same latitude index and is at the first or the last longitude index; the live slots of a donor name each of the two exactly 32 times. `send_cell`: lon_row * 128 + lat_col with lon_row < 31 and lat_col < 127. `send_target`: over the live slots of all donors that fill one receiving device, every value from 0 to 127 appears exactly once.
All inputs are finite; a program needn't handle non-finite values.
Results may differ from a plain program's by a relative error of at most 0.00002.
Values sent between devices are 32-bit elements; how exact they have to be, the bound alone decides.
A program may use at most 64 MiB of HBM per device.

v0:
```python
import jax
import jax.numpy as jnp
from jax import lax
from jax.sharding import PartitionSpec as P

TILE = 8
BLOCK = 128
HALO = 9


def with_halo(cells, sides, width):
    for axis, dim in sides:
        count = lax.axis_size(axis)
        ends = count - 1
        head = lax.slice_in_dim(cells, 0, width, axis=dim)
        tail = lax.slice_in_dim(cells, cells.shape[dim] - width, cells.shape[dim], axis=dim)
        cells = jnp.concatenate(
            [
                lax.ppermute(tail, axis, [(i, (i + 1) % count) for i in range(ends)]),
                cells,
                lax.ppermute(head, axis, [((i + 1) % count, i) for i in range(ends)]),
            ],
            axis=dim,
        )
    return cells


def lagrange(x):
    return (
        -x * (x - 1.0) * (x - 2.0) / 6.0,
        (x + 1.0) * (x - 1.0) * (x - 2.0) / 2.0,
        -(x + 1.0) * x * (x - 2.0) / 2.0,
        (x + 1.0) * x * (x - 1.0) / 6.0,
    )


def interpolate(window, frac_lon, frac_lat):
    lon_weights = lagrange(frac_lon)
    lat_weights = lagrange(frac_lat)
    summed = jnp.zeros((window.shape[0], TILE, BLOCK), jnp.float32)
    for a in range(4):
        inner_sum = jnp.zeros((window.shape[0], TILE, BLOCK), jnp.float32)
        for b in range(4):
            inner_sum = inner_sum + lat_weights[b] * window[:, a : a + TILE, b : b + BLOCK]
        summed = summed + lon_weights[a] * inner_sum
    return summed


def advect(padded, offsets, fractions, halo_width):
    tiles_lon = offsets.shape[1]
    tiles_lat = offsets.shape[2]
    channels = padded.shape[0]

    def one_row(t):

        def one_tile(u):
            start_lon = t * TILE + halo_width + offsets[0, t, u] - 1
            start_lat = u * BLOCK + halo_width + offsets[1, t, u] - 1
            window = lax.dynamic_slice(
                padded, (jnp.int32(0), start_lon, start_lat), (channels, TILE + 3, BLOCK + 3)
            )
            frac_tile = lax.dynamic_slice(
                fractions, (jnp.int32(0), t * TILE, u * BLOCK), (2, TILE, BLOCK)
            )
            return interpolate(window, frac_tile[0], frac_tile[1])

        return jax.vmap(one_tile)(jnp.arange(tiles_lat, dtype=jnp.int32))

    tiled = lax.map(one_row, jnp.arange(tiles_lon, dtype=jnp.int32))
    return tiled.transpose(2, 0, 3, 1, 4).reshape(channels, tiles_lon * TILE, tiles_lat * BLOCK)


def bilinear(base_val, lat_next, lon_next, diagonal_next, a, b):
    return (
        (1.0 - a) * (1.0 - b) * base_val
        + (1.0 - a) * b * lat_next
        + a * (1.0 - b) * lon_next
        + a * b * diagonal_next
    )


def body(fields, offsets, fractions, send_count, send_owner, send_cell, send_target, send_frac):
    local_block = fields[0]
    channels, row_count, col_count = local_block.shape
    padded = with_halo(local_block, (("lon", 1), ("lat", 2)), HALO)
    advected = advect(padded, offsets[0], fractions[0], HALO)
    slot_count = send_owner.shape[-1]
    capacity = slot_count // 2
    lon_count = lax.axis_size("lon")
    owner_lon = send_owner[0, 0, 0]
    donor_cell = send_cell[0, 0, 0]
    target = send_target[0, 0, 0]
    weights = send_frac[0, 0, 0]
    flattened = advected.reshape(channels, row_count * col_count)
    donor = bilinear(
        flattened[:, donor_cell],
        flattened[:, donor_cell + 1],
        flattened[:, donor_cell + col_count],
        flattened[:, donor_cell + col_count + 1],
        weights[0],
        weights[1],
    )
    slot_index = jnp.arange(slot_count, dtype=jnp.int32)
    is_live = slot_index < send_count[0, 0, 0]
    same_owner = (
        (owner_lon[:, None] == owner_lon[None, :])
        & (slot_index[None, :] < slot_index[:, None])
        & is_live[None, :]
    )
    position = jnp.sum(same_owner.astype(jnp.int32), axis=1)
    other_panel = 1 - lax.axis_index("panel")
    buckets = 2 * lon_count * capacity
    destination = (other_panel * lon_count + owner_lon) * capacity + position
    destination = jnp.where(is_live, destination, buckets)
    send_values = (
        jnp.zeros((buckets, channels), jnp.float32).at[destination].set(donor.T, mode="drop")
    )
    send_places = (
        jnp.full((buckets,), col_count, jnp.int32).at[destination].set(target, mode="drop")
    )
    received, recv_target = (
        lax.all_to_all(
            send_values.reshape(2 * lon_count, capacity, channels),
            ("panel", "lon"),
            split_axis=0,
            concat_axis=0,
            tiled=True,
        ),
        lax.all_to_all(
            send_places.reshape(2 * lon_count, capacity),
            ("panel", "lon"),
            split_axis=0,
            concat_axis=0,
            tiled=True,
        ),
    )
    received = received.reshape(-1, channels)
    recv_target = recv_target.reshape(-1)
    rim_values = (
        jnp.zeros((col_count, channels), jnp.float32).at[recv_target].set(received, mode="drop").T
    )
    lon_index = lax.axis_index("lon")
    first_row = jnp.where(lon_index == 0, rim_values, advected[:, 0, :])
    last_row = jnp.where(lon_index == lon_count - 1, rim_values, advected[:, row_count - 1, :])
    advected = advected.at[:, 0, :].set(first_row).at[:, row_count - 1, :].set(last_row)
    return advected[None]


def solution(mesh):
    placed = (
        P("panel", None, "lon", "lat"),
        P("panel", None, "lon", "lat"),
        P("panel", None, "lon", "lat"),
        P("panel", "lon", "lat"),
        P("panel", "lon", "lat", None),
        P("panel", "lon", "lat", None),
        P("panel", "lon", "lat", None),
        P("panel", "lon", "lat", None, None),
    )
    return jax.shard_map(
        body, mesh=mesh, in_specs=placed, out_specs=P("panel", None, "lon", "lat"), check_vma=False
    )
```

profile of v0, /device:TPU:0, one launch (start us, length us, event | category | flops | bytes accessed | tf_op | source)
XLA Modules:
  0.0 84.1 jit_solution(4624009519742526504)
XLA Ops:
  0.0 1.3 %copy.79 = f32[1,24,32,128]{3,1,2,0:T(8,128)S(1)} copy(f32[1,24,32,128]{3,2,1,0:T(8,128)} %param.14) | data formatting | bytes 786432 | tf_op args[0]
  1.3 4.8 %collective-permute-start = (f32[24,9,128]{2,0,1:T(8,128)S(1)}, f32[24,9,128]{2,0,1:T(8,128)S(1)}, u32[]{:S(2)}, u32[]{:S(2)}) collective-permute-start(f32[24,9,128]{2,0,1:T(8,128)S(1)} %get-tuple-element.289), channel_id=1, source_target_pairs={{0,2},{2,4},{4,6},{6,8},{8,10},{10,12},{12,14},{1,3},{3,5},{5,7},{... | collective-permute-start | bytes 331784 | tf_op jit(solution)/shard_map/ppermute | solution.py:19
  6.2 1.3 %collective-permute-start.1 = (f32[24,9,128]{2,0,1:T(8,128)S(1)}, f32[24,9,128]{2,0,1:T(8,128)S(1)}, u32[]{:S(2)}, u32[]{:S(2)}) collective-permute-start(f32[24,9,128]{2,0,1:T(8,128)S(1)} %get-tuple-element.290), channel_id=1, source_target_pairs={{2,0},{4,2},{6,4},{8,6},{10,8},{12,10},{14,12},{3,1},{5,3},{7,5},{... | collective-permute-start | bytes 331784 | tf_op jit(solution)/shard_map/ppermute | solution.py:21
  8.3 0.9 %scatter_custom_fusion = s32[512]{0:T(512)S(1)} fusion(s32[64]{0:T(128)S(1)} %fusion.68, s32[64]{0:T(128)} %bitcast.168, s32[]{:T(128)} %constant.265.clone.1), kind=kCustom, calls=%fused_computation.117 | custom fusion | bytes 2560 | tf_op jit(solution)/shard_map/scatter | solution.py:119
  9.2 0.7 all_to_all.9
  9.9 7.1 %all-to-all-start = ((s32[16,1,32]{2,1,0:T(1,128)}), s32[16,1,32]{2,1,0:T(1,128)S(1)}, u32[]{:S(2)}, u32[]{:S(2)}) async-start(s32[16,1,32]{2,1,0:T(1,128)} %all_to_all.9), calls=%async_computation | async-start | bytes 16384 | tf_op jit(solution)/shard_map/all_to_all | solution.py:129
  17.1 6.2 %all-to-all-done = s32[16,1,32]{2,1,0:T(1,128)S(1)} async-done(((s32[16,1,32]{2,1,0:T(1,128)}), s32[16,1,32]{2,1,0:T(1,128)S(1)}, u32[]{:S(2)}, u32[]{:S(2)}) %all-to-all-start) | async-done | bytes 2080 | tf_op jit(solution)/shard_map/all_to_all | solution.py:129
  25.2 3.4 %collective-permute-start.2 = (f32[24,50,9]{1,0,2:T(8,128)S(1)}, f32[24,50,9]{1,0,2:T(8,128)S(1)}, u32[]{:S(2)}, u32[]{:S(2)}) collective-permute-start(f32[24,50,9]{1,0,2:T(8,128)S(1)} %copy.73), channel_id=1, source_target_pairs={{0,1},{2,3},{4,5},{6,7},{8,9},{10,11},{12,13},{14,15},{16,17},{18,... | collective-permute-start | bytes 129608 | tf_op jit(solution)/shard_map/ppermute | solution.py:19
  28.9 1.3 %collective-permute-start.3 = (f32[24,50,9]{1,0,2:T(8,128)S(1)}, f32[24,50,9]{1,0,2:T(8,128)S(1)}, u32[]{:S(2)}, u32[]{:S(2)}) collective-permute-start(f32[24,50,9]{1,0,2:T(8,128)S(1)} %copy.74), channel_id=1, source_target_pairs={{1,0},{3,2},{5,4},{7,6},{9,8},{11,10},{13,12},{15,14},{17,16},{19,... | collective-permute-start | bytes 129608 | tf_op jit(solution)/shard_map/ppermute | solution.py:21
  30.2 0.7 collective-permute-done.2
  31.3 4.3 %collective-permute-done.3 = f32[24,50,9]{1,0,2:T(8,128)S(1)} collective-permute-done((f32[24,50,9]{1,0,2:T(8,128)S(1)}, f32[24,50,9]{1,0,2:T(8,128)S(1)}, u32[]{:S(2)}, u32[]{:S(2)}) %collective-permute-start.3) | collective-permute-done | bytes 43232 | tf_op jit(solution)/shard_map/ppermute | solution.py:21
  36.6 28.6 %while.21 = (s32[]{:T(128)}, f32[4,1,24,8,128]{4,3,2,1,0:T(8,128)S(1)}, s32[4]{0:T(128)S(1)}, f32[2,32,128]{2,1,0:T(8,128)}, s32[2,4,1]{1,2,0:T(1,128)S(1)}, /*i...) while((s32[]{:T(128)}, ...), condition=%wide.region_1.2_spmd, body=%wide.region_0.1_spmd.sunk | while | flops 894995 | bytes 2315025 | solution.py:69
  42.6 0.7 dynamic-slice_bitcast_fusion.2
  49.8 0.7 dynamic-slice_bitcast_fusion.2
  57.0 0.7 dynamic-slice_bitcast_fusion.2
  64.1 0.7 dynamic-slice_bitcast_fusion.2
  65.9 1.4 %scatter_custom_fusion.1 = f32[512,24]{1,0:T(8,128)S(1)} fusion(s32[64]{0:T(128)S(1)} %fusion.68, f32[]{:T(128)} %constant.262.clone.1, f32[64]{0:T(128)S(1)} %get-tuple-element.294, f32[64]{0:T(128)S(1)} %get-tuple-element.293, f32[64]{0:T(128)S(1)} %get-tuple-element.292, f32[64]{0:T(128)S(1)} %get-tuple-element.291, f32[24,4096]{0,1:T(8,128)S(1)} %bitcast.154, ...), kind=kCustom, calls=%fused_computation.81 | custom fusion | flops 10752 | bytes 8456196 | tf_op jit(solution)/shard_map/scatter | solution.py:116
  67.4 0.8 reshape.676
  68.2 3.5 %all-to-all-start.1 = ((f32[16,1,768]{2,1,0:T(1,128)}), f32[16,1,768]{2,1,0:T(1,128)S(1)}, u32[]{:S(2)}, u32[]{:S(2)}) async-start(f32[16,1,768]{2,1,0:T(1,128)} %reshape.676), calls=%async_computation.1 | async-start | bytes 98304 | tf_op jit(solution)/shard_map/all_to_all | solution.py:122
  71.7 6.5 %all-to-all-done.1 = f32[16,1,768]{2,1,0:T(1,128)S(1)} async-done(((f32[16,1,768]{2,1,0:T(1,128)}), f32[16,1,768]{2,1,0:T(1,128)S(1)}, u32[]{:S(2)}, u32[]{:S(2)}) %all-to-all-start.1) | async-done | bytes 49184 | tf_op jit(solution)/shard_map/all_to_all | solution.py:122
  78.8 0.8 reduce.8
  79.8 1.7 %scatter_custom_fusion.2 = f32[128,24]{1,0:T(8,128)S(1)} fusion(s32[512]{0:T(512)S(1)} %bitcast.167, f32[512,24]{1,0:T(8,128)S(1)} %bitcast.163, f32[]{:T(128)} %constant.262.clone.1), kind=kCustom, calls=%fused_computation.98 | custom fusion | bytes 12292 | tf_op jit(solution)/shard_map/scatter | solution.py:140
  81.7 0.7 copy-done
  82.5 1.6 %scatter.35 = f32[1,24,32,128]{3,2,1,0:T(8,128)} dynamic-update-slice(f32[1,24,32,128]{3,2,1,0:T(8,128)} %copy-done, f32[1,24,1,128]{3,2,1,0:T(1,128)S(1)} %copy.69, s32[]{:T(128)} %constant.261.clone.1, s32[]{:T(128)} %constant.261.clone.1, s32[]{:T(128)} %constant.278.clone.1, s32[]{:T(128)} %constant.261.clone.1) | dynamic-update-slice | bytes 24580 | tf_op jit(solution)/shard_map/scatter | solution.py:145
  (66 shorter events, 13.0 us)
Async XLA Ops:
  0.0 8.1 %copy-start.2 = (s32[1,1,1,64]{3,2,1,0:T(1,128)S(1)}, s32[1,1,1,64]{3,2,1,0:T(1,128)}, u32[]{:S(2)}) copy-start(s32[1,1,1,64]{3,2,1,0:T(1,128)} %param.18) | copy-start | bytes 772
  0.0 17.0 %copy-start.4 = (s32[1,1,1,64]{3,2,1,0:T(1,128)S(1)}, s32[1,1,1,64]{3,2,1,0:T(1,128)}, u32[]{:S(2)}) copy-start(s32[1,1,1,64]{3,2,1,0:T(1,128)} %param.19) | copy-start | bytes 772
  0.0 17.0 %copy-start.3 = (f32[1,1,1,2,64]{4,3,2,1,0:T(2,128)S(1)}, f32[1,1,1,2,64]{4,3,2,1,0:T(2,128)}, u32[]{:S(2)}) copy-start(f32[1,1,1,2,64]{4,3,2,1,0:T(2,128)} %param.21) | copy-start | bytes 1540
  1.3 23.3 %collective-permute-start = (f32[24,9,128]{2,0,1:T(8,128)S(1)}, f32[24,9,128]{2,0,1:T(8,128)S(1)}, u32[]{:S(2)}, u32[]{:S(2)}) collective-permute-start(f32[24,9,128]{2,0,1:T(8,128)S(1)} %get-tuple-element.289), channel_id=1, source_target_pairs={{0,2},{2,4},{4,6},{6,8},{8,10},{10,12},{12,14},{1,3},{3,5},{5,7},{... | collective-permute-start | bytes 331784 | tf_op jit(solution)/shard_map/ppermute | solution.py:19
  6.2 18.4 %collective-permute-start.1 = (f32[24,9,128]{2,0,1:T(8,128)S(1)}, f32[24,9,128]{2,0,1:T(8,128)S(1)}, u32[]{:S(2)}, u32[]{:S(2)}) collective-permute-start(f32[24,9,128]{2,0,1:T(8,128)S(1)} %get-tuple-element.290), channel_id=1, source_target_pairs={{2,0},{4,2},{6,4},{8,6},{10,8},{12,10},{14,12},{3,1},{5,3},{7,5},{... | collective-permute-start | bytes 331784 | tf_op jit(solution)/shard_map/ppermute | solution.py:21
  9.9 13.4 %all-to-all-start = ((s32[16,1,32]{2,1,0:T(1,128)}), s32[16,1,32]{2,1,0:T(1,128)S(1)}, u32[]{:S(2)}, u32[]{:S(2)}) async-start(s32[16,1,32]{2,1,0:T(1,128)} %all_to_all.9), calls=%async_computation | async-start | bytes 16384 | tf_op jit(solution)/shard_map/all_to_all | solution.py:129
  25.2 5.7 %collective-permute-start.2 = (f32[24,50,9]{1,0,2:T(8,128)S(1)}, f32[24,50,9]{1,0,2:T(8,128)S(1)}, u32[]{:S(2)}, u32[]{:S(2)}) collective-permute-start(f32[24,50,9]{1,0,2:T(8,128)S(1)} %copy.73), channel_id=1, source_target_pairs={{0,1},{2,3},{4,5},{6,7},{8,9},{10,11},{12,13},{14,15},{16,17},{18,... | collective-permute-start | bytes 129608 | tf_op jit(solution)/shard_map/ppermute | solution.py:19
  28.9 6.6 %collective-permute-start.3 = (f32[24,50,9]{1,0,2:T(8,128)S(1)}, f32[24,50,9]{1,0,2:T(8,128)S(1)}, u32[]{:S(2)}, u32[]{:S(2)}) collective-permute-start(f32[24,50,9]{1,0,2:T(8,128)S(1)} %copy.74), channel_id=1, source_target_pairs={{1,0},{3,2},{5,4},{7,6},{9,8},{11,10},{13,12},{15,14},{17,16},{19,... | collective-permute-start | bytes 129608 | tf_op jit(solution)/shard_map/ppermute | solution.py:21
  35.9 0.7 copy-start.1
  68.2 10.1 %all-to-all-start.1 = ((f32[16,1,768]{2,1,0:T(1,128)}), f32[16,1,768]{2,1,0:T(1,128)S(1)}, u32[]{:S(2)}, u32[]{:S(2)}) async-start(f32[16,1,768]{2,1,0:T(1,128)} %reshape.676), calls=%async_computation.1 | async-start | bytes 98304 | tf_op jit(solution)/shard_map/all_to_all | solution.py:122
  81.7 0.7 copy-start
where the time goes:
time: 84.9 us; the launch traced here: 84.1 us
  starting transfers between devices  21.4 us (25%)
  local copies, waits for them, and re-layouts  20.4 us (24%)
  loops' own time  18.3 us (22%)
  waiting for transfers between devices  17.7 us (21%)
  other arithmetic  5.2 us (6%)
  between operations  0.95 us (1%)
    another operation x1, loops' own time, advect(): tiled = lax.map(one_row, jnp.arange(tiles_lon, dtype=jnp.int32))  18.3 us
    ppermute x2, starting transfers between devices, with_halo(): lax.ppermute(tail, axis, [(i, (i + 1) % count) for i in range(ends)])  8.28 us
    all_to_all x1, starting transfers between devices, body(): lax.all_to_all(send_places.reshape(2 * lon_count, capacity), ('panel', 'l...  7.06 us
    all_to_all x1, waiting for transfers between devices, body(): lax.all_to_all(send_values.reshape(2 * lon_count, capacity, channels), ('...  6.54 us
    all_to_all x1, waiting for transfers between devices, body(): lax.all_to_all(send_places.reshape(2 * lon_count, capacity), ('panel', 'l...  6.22 us
    ppermute x2, waiting for transfers between devices, with_halo(): lax.ppermute(head, axis, [((i + 1) % count, i) for i in range(ends)])  4.3 us
    unnamed x15, local copies, waits for them, and re-layouts  3.63 us
    all_to_all x1, starting transfers between devices, body(): lax.all_to_all(send_values.reshape(2 * lon_count, capacity, channels), ('...  3.5 us
  transfers between devices with their start and end apart: 6, of which 4 were waited for; matrix products, arithmetic and copies ran while one was open for 4% of the time, Pallas kernels for 0%

commit v1 on v0

v1 whole, which is shorter than its diff:
```python
import functools

import jax
import jax.numpy as jnp
from jax import lax
from jax.experimental import pallas as pl
from jax.experimental.pallas import tpu as pltpu
from jax.sharding import PartitionSpec as P

TILE = 8
LOW = 8
HIGH = 9
STRIP = 16
PER = 128 // STRIP
MESH = pl.DeviceIdType.MESH


def lagrange(x):
    return (
        -x * (x - 1.0) * (x - 2.0) * (1.0 / 6.0),
        (x + 1.0) * (x - 1.0) * (x - 2.0) * 0.5,
        -(x + 1.0) * x * (x - 2.0) * 0.5,
        (x + 1.0) * x * (x - 1.0) * (1.0 / 6.0),
    )


def kernel(
    lon_count, lat_count, rows, channels, slots,
    offsets, count, owner, cell, target, frac,
    x_ref, frac_ref, out_ref,
    ext, pack_l, pack_r, from_r, from_l, halo, weights, rim_out, rim_in,
    send_sem, recv_sem, rim_send, rim_recv,
):
    p = lax.axis_index("panel")
    i = lax.axis_index("lon")
    j = lax.axis_index("lat")
    groups = rows // PER
    has_prev, has_next = i > 0, i < lon_count - 1
    has_left, has_right = j > 0, j < lat_count - 1
    is_rim = jnp.logical_or(i == 0, i == lon_count - 1)

    own = LOW
    plan = [
        (ext.at[pl.ds(own, HIGH)], ext.at[pl.ds(own + rows, HIGH)], -1, 0, has_prev),
        (ext.at[pl.ds(own + rows - LOW, LOW)], ext.at[pl.ds(0, LOW)], 1, 0, has_next),
        (pack_l, from_r.at[pl.ds(1, groups)], 0, -1, has_left),
        (pack_r, from_l.at[pl.ds(1, groups)], 0, 1, has_right),
        (pack_l.at[pl.ds(0, 2)], from_r.at[pl.ds(1 + groups, 2)], -1, -1, has_prev & has_left),
        (pack_l.at[pl.ds(groups - 1, 1)], from_r.at[pl.ds(0, 1)], 1, -1, has_next & has_left),
        (pack_r.at[pl.ds(0, 2)], from_l.at[pl.ds(1 + groups, 2)], -1, 1, has_prev & has_right),
        (pack_r.at[pl.ds(groups - 1, 1)], from_l.at[pl.ds(0, 1)], 1, 1, has_next & has_right),
    ]
    arrives = [
        has_next, has_prev, has_right, has_left,
        has_next & has_right, has_prev & has_right, has_next & has_left, has_prev & has_left,
    ]

    barrier = pltpu.get_barrier_semaphore()
    waits = jnp.int32(0)
    for _, _, di, dj, there in plan:
        @pl.when(there)
        def _(di=di, dj=dj):
            pl.semaphore_signal(barrier, inc=1, device_id=(p, i + di, j + dj), device_id_type=MESH)
        waits = waits + there.astype(jnp.int32)

    @pl.when(is_rim)
    def _():
        def greet(m, carry):
            pl.semaphore_signal(barrier, inc=1, device_id=(1 - p, m, j), device_id_type=MESH)
            return carry
        lax.fori_loop(0, lon_count, greet, 0)

    @pl.when(jnp.logical_not(is_rim))
    def _():
        for m in (0, lon_count - 1):
            pl.semaphore_signal(barrier, inc=1, device_id=(1 - p, m, j), device_id_type=MESH)

    waits = waits + jnp.where(is_rim, lon_count, 2)

    def clear(ref, start, size):
        ref[pl.ds(start, size)] = jnp.zeros((size,) + ref.shape[1:], jnp.float32)

    @pl.when(jnp.logical_not(has_prev))
    def _():
        clear(ext, 0, LOW)
        clear(from_r, 0, 1)
        clear(from_l, 0, 1)

    @pl.when(jnp.logical_not(has_next))
    def _():
        clear(ext, own + rows, HIGH)
        clear(from_r, 1 + groups, 2)
        clear(from_l, 1 + groups, 2)

    @pl.when(jnp.logical_not(has_right))
    def _():
        clear(from_r, 0, groups + 3)

    @pl.when(jnp.logical_not(has_left))
    def _():
        clear(from_l, 0, groups + 3)

    lane = lax.broadcasted_iota(jnp.int32, (8, 128), 1)
    strip = lane // STRIP

    def prepare(g, carry):
        for c in range(channels // 8):
            left = jnp.zeros((8, 128), jnp.float32)
            right = jnp.zeros((8, 128), jnp.float32)
            for m in range(PER):
                row = g * PER + m
                v = x_ref[pl.ds(c * 8 * rows + row, 8, stride=rows), :]
                ext[own + row, pl.ds(c * 8, 8), :] = v
                rolled = pltpu.roll(v, STRIP * m, 1) if m else v
                left = jnp.where(strip == m, rolled, left)
                right = jnp.where(strip == (m + PER - 1) % PER, rolled, right)
            pack_l[g, pl.ds(c * 8, 8), :] = left
            pack_r[g, pl.ds(c * 8, 8), :] = right
        at = pl.ds(pl.multiple_of(g * 8, 8), 8)
        for axis in range(2):
            for n, w in enumerate(lagrange(frac_ref[axis, at, :])):
                weights[4 * axis + n, at, :] = w
        return carry

    lax.fori_loop(0, groups, prepare, 0)

    pl.semaphore_wait(barrier, waits)

    copies = []
    for n, (src, dst, di, dj, there) in enumerate(plan):
        copy = pltpu.make_async_remote_copy(
            src_ref=src, dst_ref=dst, send_sem=send_sem.at[n], recv_sem=recv_sem.at[n],
            device_id=(p, i + di, j + dj), device_id_type=MESH,
        )
        copies.append(copy)
        pl.when(there)(copy.start)
    for n, copy in enumerate(copies):
        pl.when(arrives[n])(copy.wait_recv)

    def unpack_row(g, m, c):
        at = pl.ds(c * 8, 8)
        a, b = from_r[g, at, :], from_l[g, at, :]
        if m:
            a = pltpu.roll(a, 128 - STRIP * m, 1)
            b = pltpu.roll(b, 128 - STRIP * m, 1)
        halo[g * PER + m, at, :] = jnp.where(lane < 64, a, b)

    def unpack(g, carry):
        for c in range(channels // 8):
            for m in range(PER):
                unpack_row(g, m, c)
        return carry

    lax.fori_loop(0, groups + 2, unpack, 0)
    for c in range(channels // 8):
        unpack_row(groups + 2, 0, c)

    wide = lax.broadcasted_iota(jnp.int32, (channels, 128), 1)

    def tile(t, carry):
        start = t * TILE + LOW - 1 + offsets[0, 0, t]
        shift = offsets[1, 0, t]
        inside, turn = [], []
        for b in range(4):
            k = shift + (b - 1)
            inside.append((wide >= k) & (wide < 128 + k))
            turn.append((256 - k) & 127)
        sums = [None] * TILE
        for q in range(TILE + 3):
            main, edge = ext[start + q], halo[start + q]
            shifted = [pltpu.roll(jnp.where(inside[b], main, edge), turn[b], 1) for b in range(4)]
            for a in range(4):
                r = q - a
                if not 0 <= r < TILE:
                    continue
                at = pl.ds(t * TILE + r, 1)
                inner = weights[4, at, :] * shifted[0]
                for b in range(1, 4):
                    inner = inner + weights[4 + b, at, :] * shifted[b]
                term = weights[a, at, :] * inner
                sums[r] = term if sums[r] is None else sums[r] + term
                if a == 3:
                    out_ref[t * TILE + r] = sums[r]
        return carry

    lax.fori_loop(0, rows // TILE, tile, 0)

    live = count[0, 0, 0]

    def donate(k, carry):
        first, last = carry
        place = cell[0, 0, 0, k]
        row, col = place >> 7, place & 127
        to = target[0, 0, 0, k]
        a, b = frac[0, 0, 0, 0, k], frac[0, 0, 0, 1, k]
        to_first = owner[0, 0, 0, k] == 0
        near, far = out_ref[row], out_ref[row + 1]
        here = (256 + to - col) & 127
        beyond = (255 + to - col) & 127
        near = (1.0 - b) * pltpu.roll(near, here, 1) + b * pltpu.roll(near, beyond, 1)
        far = (1.0 - b) * pltpu.roll(far, here, 1) + b * pltpu.roll(far, beyond, 1)
        value = (1.0 - a) * near + a * far
        to = jnp.where(k < live, to, 128)
        first = jnp.where(wide == jnp.where(to_first, to, 128), value, first)
        last = jnp.where(wide == jnp.where(to_first, 128, to), value, last)
        return first, last

    zero = jnp.zeros((channels, 128), jnp.float32)
    first, last = lax.fori_loop(0, slots, donate, (zero, zero))
    rim_out[0] = first
    rim_out[1] = last

    sends = []
    for n, m in enumerate((0, lon_count - 1)):
        copy = pltpu.make_async_remote_copy(
            src_ref=rim_out.at[n], dst_ref=rim_in.at[i], send_sem=rim_send.at[n],
            recv_sem=rim_recv.at[i], device_id=(1 - p, m, j), device_id_type=MESH,
        )
        copy.start()
        sends.append(copy)

    @pl.when(is_rim)
    def _():
        total = zero
        for m in range(lon_count):
            pltpu.make_async_remote_copy(
                src_ref=rim_out.at[0], dst_ref=rim_in.at[m], send_sem=rim_send.at[0],
                recv_sem=rim_recv.at[m], device_id=(1 - p, m, j), device_id_type=MESH,
            ).wait_recv()
            total = total + rim_in[m]
        out_ref[jnp.where(i == 0, 0, rows - 1)] = total

    for n, copy in enumerate(copies):
        pl.when(plan[n][4])(copy.wait_send)
    for copy in sends:
        copy.wait_send()


def body(fields, offsets, fractions, send_count, send_owner, send_cell, send_target, send_frac):
    _, channels, rows, columns = fields.shape
    lon_count, lat_count = lax.axis_size("lon"), lax.axis_size("lat")
    slots = send_owner.shape[-1]
    groups = rows // PER
    smem = pl.BlockSpec(memory_space=pltpu.SMEM)
    vmem = pl.BlockSpec(memory_space=pltpu.VMEM)
    f32 = jnp.float32
    out = pl.pallas_call(
        functools.partial(kernel, lon_count, lat_count, rows, channels, slots),
        out_shape=jax.ShapeDtypeStruct((rows, channels, columns), f32),
        in_specs=[smem] * 6 + [vmem] * 2,
        out_specs=vmem,
        scratch_shapes=[
            pltpu.VMEM((LOW + rows + HIGH, channels, columns), f32),
            pltpu.VMEM((groups, channels, columns), f32),
            pltpu.VMEM((groups, channels, columns), f32),
            pltpu.VMEM((groups + 3, channels, columns), f32),
            pltpu.VMEM((groups + 3, channels, columns), f32),
            pltpu.VMEM((LOW + rows + HIGH, channels, columns), f32),
            pltpu.VMEM((8, rows, columns), f32),
            pltpu.VMEM((2, channels, columns), f32),
            pltpu.VMEM((lon_count, channels, columns), f32),
            pltpu.SemaphoreType.DMA((8,)),
            pltpu.SemaphoreType.DMA((8,)),
            pltpu.SemaphoreType.DMA((2,)),
            pltpu.SemaphoreType.DMA((lon_count,)),
        ],
        compiler_params=pltpu.CompilerParams(
            collective_id=0, has_side_effects=True, vmem_limit_bytes=24 * 1024 * 1024
        ),
    )(
        offsets.reshape(2, 1, rows // TILE), send_count, send_owner, send_cell, send_target, send_frac,
        fields.reshape(channels * rows, columns), fractions.reshape(2, rows, columns),
    )
    return out.transpose(1, 0, 2)[None]


def solution(mesh):
    placed = (
        P("panel", None, "lon", "lat"),
        P("panel", None, "lon", "lat"),
        P("panel", None, "lon", "lat"),
        P("panel", "lon", "lat"),
        P("panel", "lon", "lat", None),
        P("panel", "lon", "lat", None),
        P("panel", "lon", "lat", None),
        P("panel", "lon", "lat", None, None),
    )
    return jax.shard_map(
        body, mesh=mesh, in_specs=placed, out_specs=P("panel", None, "lon", "lat"), check_vma=False
    )
```

time: 84.9 us -> 28.6 us (0.34)
  Pallas kernels: 0 us -> 24.4 us
  starting transfers between devices: 21.4 us -> 0 us
  loops' own time: 18.3 us -> 0 us
  waiting for transfers between devices: 17.7 us -> 0 us
  local copies, waits for them, and re-layouts: 20.4 us -> 3.26 us
  other arithmetic: 5.2 us -> 0 us
    pallas_call x0 -> x1, Pallas kernels: none -> 24.4 us  [body(): pl.pallas_call(functools.partial(kernel, lon_count, lat_count, rows, chan...]
    another operation x1 -> x0, loops' own time: 18.3 us -> none  [advect(): tiled = lax.map(one_row, jnp.arange(tiles_lon, dtype=jnp.int32))]
    all_to_all x2 -> x0, waiting for transfers between devices: 12.8 us -> none  [the longest x1 6.54 us: body(): lax.all_to_all(send_values.reshape(2 * lon_count, capacity, channels), ('...]
    ppermute x4 -> x0, starting transfers between devices: 10.9 us -> none  [the longest x2 8.28 us: with_halo(): lax.ppermute(tail, axis, [(i, (i + 1) % count) for i in range(ends)])]
    all_to_all x2 -> x0, starting transfers between devices: 10.6 us -> none  [the longest x1 7.06 us: body(): lax.all_to_all(send_places.reshape(2 * lon_count, capacity), ('panel', 'l...]
    ppermute x4 -> x0, waiting for transfers between devices: 4.98 us -> none  [the longest x2 4.3 us: with_halo(): lax.ppermute(head, axis, [((i + 1) % count, i) for i in range(ends)])]
    scatter x4 -> x0, local copies, waits for them, and re-layouts: 4.29 us -> none  [the longest x1 1.73 us: body(): jnp.zeros((col_count, channels), jnp.float32).at[recv_target]]
    while x12 -> x0, local copies, waits for them, and re-layouts: 3.59 us -> none  [the longest x4 2.63 us: one_tile(): start_lat = u * BLOCK + halo_width + offsets[1, t, u] - 1]
  transfers between devices with their start and end apart: 6 -> 0, of which waited for: 4 -> 0; matrix products, arithmetic and copies ran while one was open for 4% -> 0% of each run, Pallas kernels for 0% -> 0%
where the time goes in v1:
time: 28.6 us; the launch traced here: 28.4 us
  Pallas kernels  24.4 us (85%)
  local copies, waits for them, and re-layouts  3.26 us (11%)
  between operations  0.7 us (2%)
    pallas_call x1, Pallas kernels, body(): pl.pallas_call(functools.partial(kernel, lon_count, lat_count, rows, chan...  24.4 us
    unnamed x14, local copies, waits for them, and re-layouts  2.44 us
    broadcast_in_dim x1, local copies, waits for them, and re-layouts, body(): return out.transpose(1, 0, 2)[None]  0.82 us

profile of v1, /device:TPU:0, one launch (start us, length us, event | category | flops | bytes accessed | tf_op | source)
XLA Modules:
  0.0 28.4 jit_solution(9337323408134374139)
XLA Ops:
  0.7 0.0 copy-start.3
  0.7 0.0 copy-start.5
  0.7 0.0 copy-start.6
  0.7 0.0 copy-start.2
  0.7 0.0 copy-start.4
  0.7 0.6 %copy-done.3 = f32[1,1,1,2,64]{4,3,2,1,0:T(2,128)S(1)} copy-done((f32[1,1,1,2,64]{4,3,2,1,0:T(2,128)S(1)}, f32[1,1,1,2,64]{4,3,2,1,0:T(2,128)}, u32[]{:S(2)}) %copy-start.3) | copy-done | bytes 536
  1.3 0.0 copy-done.5
  1.3 0.0 copy-done.6
  1.3 0.0 copy-done.2
  1.4 0.0 copy-done.4
  1.4 0.0 copy-start
  1.4 1.0 %copy-done = f32[1,24,32,128]{3,2,1,0:T(8,128)S(1)} copy-done((f32[1,24,32,128]{3,2,1,0:T(8,128)S(1)}, f32[1,24,32,128]{3,2,1,0:T(8,128)}, u32[]{:S(2)}) %copy-start) | copy-done | bytes 393240
  2.4 0.0 copy-start.1
  2.4 0.8 %copy-done.1 = f32[1,2,32,128]{3,2,1,0:T(8,128)S(1)} copy-done((f32[1,2,32,128]{3,2,1,0:T(8,128)S(1)}, f32[1,2,32,128]{3,2,1,0:T(8,128)}, u32[]{:S(2)}) %copy-start.1) | copy-done | bytes 32792
  3.1 24.4 %shard_map.82 = f32[32,24,128]{2,1,0:T(8,128)S(1)} custom-call(s32[2,1,4]{2,1,0:T(1,128)S(1)} %bitcast.11, s32[1,1,1]{2,1,0:T(1,128)S(6)} %copy.11.count, s32[1,1,1,64]{3,2,1,0:T(1,128)S(1)} %copy-done.4, s32[1,1,1,64]{3,2,1,0:T(1,128)S(1)} %copy-done.5, s32[1,1,1,64]{3,2,1,0:T(1,128)S(1)} %copy-done.6, f32[1,1,1,2,64]{4,3,2,1,0:T(2,128)S(1)} %copy-done.3, ...), custom_call_target="tpu_custom_call" | custom-call | tf_op jit(solution)/shard_map/pallas_call | solution.py:247
  27.5 0.8 %copy.10 = f32[1,24,32,128]{3,2,1,0:T(8,128)} copy(f32[1,24,32,128]{3,1,2,0:T(8,128)S(1)} %bitcast.8) | data formatting | bytes 786432 | tf_op jit(solution)/shard_map/broadcast_in_dim | solution.py:274
Async XLA Ops:
  0.7 0.7 %copy-start.3 = (f32[1,1,1,2,64]{4,3,2,1,0:T(2,128)S(1)}, f32[1,1,1,2,64]{4,3,2,1,0:T(2,128)}, u32[]{:S(2)}) copy-start(f32[1,1,1,2,64]{4,3,2,1,0:T(2,128)} %frac.1) | copy-start | bytes 1540
  0.7 0.7 %copy-start.5 = (s32[1,1,1,64]{3,2,1,0:T(1,128)S(1)}, s32[1,1,1,64]{3,2,1,0:T(1,128)}, u32[]{:S(2)}) copy-start(s32[1,1,1,64]{3,2,1,0:T(1,128)} %cell.1) | copy-start | bytes 772
  0.7 0.7 %copy-start.6 = (s32[1,1,1,64]{3,2,1,0:T(1,128)S(1)}, s32[1,1,1,64]{3,2,1,0:T(1,128)}, u32[]{:S(2)}) copy-start(s32[1,1,1,64]{3,2,1,0:T(1,128)} %target.1) | copy-start | bytes 772
  0.7 0.7 %copy-start.2 = (s32[1,2,4,1]{2,3,1,0:T(1,128)S(1)}, s32[1,2,4,1]{2,3,1,0:T(1,128)}, u32[]{:S(2)}) copy-start(s32[1,2,4,1]{2,3,1,0:T(1,128)} %param.9) | copy-start | bytes 100
  0.7 0.7 %copy-start.4 = (s32[1,1,1,64]{3,2,1,0:T(1,128)S(1)}, s32[1,1,1,64]{3,2,1,0:T(1,128)}, u32[]{:S(2)}) copy-start(s32[1,1,1,64]{3,2,1,0:T(1,128)} %owner.1) | copy-start | bytes 772
  1.4 1.0 %copy-start = (f32[1,24,32,128]{3,2,1,0:T(8,128)S(1)}, f32[1,24,32,128]{3,2,1,0:T(8,128)}, u32[]{:S(2)}) copy-start(f32[1,24,32,128]{3,2,1,0:T(8,128)} %param.8) | copy-start | bytes 1179652
  2.4 0.8 %copy-start.1 = (f32[1,2,32,128]{3,2,1,0:T(8,128)S(1)}, f32[1,2,32,128]{3,2,1,0:T(8,128)}, u32[]{:S(2)}) copy-start(f32[1,2,32,128]{3,2,1,0:T(8,128)} %param.10) | copy-start | bytes 98308

commit v2 on v1

v2 whole, which is shorter than its diff:
```python
import functools

import jax
import jax.numpy as jnp
from jax import lax
from jax.experimental import pallas as pl
from jax.experimental.pallas import tpu as pltpu
from jax.sharding import PartitionSpec as P

TILE = 8
LOW = 8
HIGH = 9
STRIP = 16
PER = 128 // STRIP
MESH = pl.DeviceIdType.MESH


def lagrange(x):
    return (
        -x * (x - 1.0) * (x - 2.0) * (1.0 / 6.0),
        (x + 1.0) * (x - 1.0) * (x - 2.0) * 0.5,
        -(x + 1.0) * x * (x - 2.0) * 0.5,
        (x + 1.0) * x * (x - 1.0) * (1.0 / 6.0),
    )


def kernel(
    lon_count, lat_count, rows, channels, slots,
    offsets_hbm, count, owner_hbm, cell_hbm, target_hbm, frac_hbm, x_hbm, fractions_hbm, out_ref,
    offsets, owner, cell, target, frac, x_ref, frac_ref,
    ext, land_lo, land_hi, pack_l, pack_r, from_r, from_l, halo, weights, rim_out, rim_in,
    in_sem, send_sem, recv_sem, rim_send, rim_recv,
):
    p = lax.axis_index("panel")
    i = lax.axis_index("lon")
    j = lax.axis_index("lat")
    groups = rows // PER
    blocks = channels // 8
    own = LOW
    has_prev, has_next = i > 0, i < lon_count - 1
    has_left, has_right = j > 0, j < lat_count - 1
    is_rim = jnp.logical_or(i == 0, i == lon_count - 1)

    around = [
        (-1, 0, has_prev), (1, 0, has_next), (0, -1, has_left), (0, 1, has_right),
        (-1, -1, has_prev & has_left), (1, -1, has_next & has_left),
        (-1, 1, has_prev & has_right), (1, 1, has_next & has_right),
    ]
    barrier = pltpu.get_barrier_semaphore()
    waits = jnp.int32(0)
    for di, dj, there in around:
        @pl.when(there)
        def _(di=di, dj=dj):
            pl.semaphore_signal(barrier, inc=1, device_id=(p, i + di, j + dj), device_id_type=MESH)
        waits = waits + there.astype(jnp.int32)

    @pl.when(is_rim)
    def _():
        def greet(m, carry):
            pl.semaphore_signal(barrier, inc=1, device_id=(1 - p, m, j), device_id_type=MESH)
            return carry
        lax.fori_loop(0, lon_count, greet, 0)

    @pl.when(jnp.logical_not(is_rim))
    def _():
        for m in (0, lon_count - 1):
            pl.semaphore_signal(barrier, inc=1, device_id=(1 - p, m, j), device_id_type=MESH)

    waits = waits + jnp.where(is_rim, lon_count, 2)

    loads = [
        pltpu.make_async_copy(src, dst, in_sem.at[n])
        for n, (src, dst) in enumerate([
            (x_hbm, x_ref), (fractions_hbm, frac_ref), (offsets_hbm, offsets),
            (owner_hbm, owner), (cell_hbm, cell), (target_hbm, target), (frac_hbm, frac),
        ])
    ]
    for load in loads:
        load.start()

    def clear(ref, start, size):
        ref[pl.ds(start, size)] = jnp.zeros((size,) + ref.shape[1:], jnp.float32)

    @pl.when(jnp.logical_not(has_prev))
    def _():
        clear(land_lo, 0, LOW)
        clear(from_r, 0, 1)
        clear(from_l, 0, 1)

    @pl.when(jnp.logical_not(has_next))
    def _():
        clear(land_hi, 0, HIGH)
        clear(from_r, 1 + groups, 2)
        clear(from_l, 1 + groups, 2)

    @pl.when(jnp.logical_not(has_right))
    def _():
        clear(from_r, 0, groups + 3)

    @pl.when(jnp.logical_not(has_left))
    def _():
        clear(from_l, 0, groups + 3)

    lane = lax.broadcasted_iota(jnp.int32, (8, 128), 1)
    strip = lane // STRIP

    def turn_row(row, c):
        v = x_ref[pl.ds(c * 8 * rows + row, 8, stride=rows), :]
        ext[own + row, pl.ds(c * 8, 8), :] = v
        return v

    def pack(g):
        for c in range(blocks):
            left = jnp.zeros((8, 128), jnp.float32)
            right = jnp.zeros((8, 128), jnp.float32)
            for m in range(PER):
                v = ext[own + g * PER + m, pl.ds(c * 8, 8), :]
                rolled = pltpu.roll(v, STRIP * m, 1) if m else v
                left = jnp.where(strip == m, rolled, left)
                right = jnp.where(strip == (m + PER - 1) % PER, rolled, right)
            pack_l[g, pl.ds(c * 8, 8), :] = left
            pack_r[g, pl.ds(c * 8, 8), :] = right

    copies = []

    def send(src, dst, side):
        di, dj, there = around[side]
        n = len(copies)
        copy = pltpu.make_async_remote_copy(
            src_ref=src, dst_ref=dst, send_sem=send_sem.at[n], recv_sem=recv_sem.at[n],
            device_id=(p, i + di, j + dj), device_id_type=MESH,
        )
        arrives = [t for a, b, t in around if (a, b) == (-di, -dj)][0]
        copies.append((copy, there, arrives))
        pl.when(there)(copy.start)

    def arrive(n):
        copy, _, arrives = copies[n]
        pl.when(arrives)(copy.wait_recv)

    loads[0].wait()
    early = list(range(HIGH)) + list(range(rows - LOW, rows))
    for row in early:
        for c in range(blocks):
            turn_row(row, c)
    pl.semaphore_wait(barrier, waits)
    send(ext.at[pl.ds(own, 1)], land_hi.at[pl.ds(0, 1)], 0)
    send(ext.at[pl.ds(own + rows - LOW, LOW)], land_lo, 1)
    send(ext.at[pl.ds(own + 1, HIGH - 1)], land_hi.at[pl.ds(1, HIGH - 1)], 0)
    for row in range(HIGH, rows - LOW):
        for c in range(blocks):
            turn_row(row, c)
    for g in range(groups):
        pack(g)
    send(pack_l, from_r.at[pl.ds(1, groups)], 2)
    send(pack_r, from_l.at[pl.ds(1, groups)], 3)
    send(pack_l.at[pl.ds(0, 2)], from_r.at[pl.ds(1 + groups, 2)], 4)
    send(pack_l.at[pl.ds(groups - 1, 1)], from_r.at[pl.ds(0, 1)], 5)
    send(pack_r.at[pl.ds(0, 2)], from_l.at[pl.ds(1 + groups, 2)], 6)
    send(pack_r.at[pl.ds(groups - 1, 1)], from_l.at[pl.ds(0, 1)], 7)

    loads[1].wait()
    for g in range(groups):
        at = pl.ds(g * 8, 8)
        for axis in range(2):
            for n, w in enumerate(lagrange(frac_ref[axis, at, :])):
                weights[4 * axis + n, at, :] = w
    for load in loads[2:]:
        load.wait()

    def unpack(g, count):
        for c in range(blocks):
            at = pl.ds(c * 8, 8)
            for m in range(count):
                a, b = from_r[g, at, :], from_l[g, at, :]
                if m:
                    a = pltpu.roll(a, 128 - STRIP * m, 1)
                    b = pltpu.roll(b, 128 - STRIP * m, 1)
                halo[g * PER + m, at, :] = jnp.where(lane < 64, a, b)

    wide = lax.broadcasted_iota(jnp.int32, (channels, 128), 1)

    def tile(t):
        start = t * TILE + LOW - 1 + offsets[0, 0, t]
        shift = offsets[1, 0, t]
        inside, turn = [], []
        for b in range(4):
            k = shift + (b - 1)
            inside.append((wide >= k) & (wide < 128 + k))
            turn.append((256 - k) & 127)
        sums = [None] * TILE
        for q in range(TILE + 3):
            main, edge = ext[start + q], halo[start + q]
            shifted = [pltpu.roll(jnp.where(inside[b], main, edge), turn[b], 1) for b in range(4)]
            for a in range(4):
                r = q - a
                if not 0 <= r < TILE:
                    continue
                at = pl.ds(t * TILE + r, 1)
                inner = weights[4, at, :] * shifted[0]
                for b in range(1, 4):
                    inner = inner + weights[4 + b, at, :] * shifted[b]
                term = weights[a, at, :] * inner
                sums[r] = term if sums[r] is None else sums[r] + term
                if a == 3:
                    out_ref[t * TILE + r] = sums[r]

    tiles = rows // TILE
    for n in (3, 4):
        arrive(n)
    for g in range(1, 1 + groups):
        unpack(g, PER)
    for t in range(1, tiles - 2):
        tile(t)
    for n in (0, 5, 7):
        arrive(n)
    unpack(1 + groups, PER)
    unpack(2 + groups, 1)
    ext[own + rows] = land_hi[0]
    tile(tiles - 2)
    for n in (1, 6, 8):
        arrive(n)
    unpack(0, PER)
    ext[pl.ds(0, LOW)] = land_lo[...]
    tile(0)
    arrive(2)
    ext[pl.ds(own + rows + 1, HIGH - 1)] = land_hi[pl.ds(1, HIGH - 1)]
    tile(tiles - 1)

    live = count[0, 0, 0]

    def donate(k, carry):
        first, last = carry
        place = cell[0, 0, 0, k]
        row, col = place >> 7, place & 127
        to = target[0, 0, 0, k]
        a, b = frac[0, 0, 0, 0, k], frac[0, 0, 0, 1, k]
        to_first = owner[0, 0, 0, k] == 0
        mixed = (1.0 - a) * out_ref[row] + a * out_ref[row + 1]
        here = (256 + to - col) & 127
        beyond = (255 + to - col) & 127
        value = (1.0 - b) * pltpu.roll(mixed, here, 1) + b * pltpu.roll(mixed, beyond, 1)
        to = jnp.where(k < live, to, 128)
        first = jnp.where(wide == jnp.where(to_first, to, 128), value, first)
        last = jnp.where(wide == jnp.where(to_first, 128, to), value, last)
        return first, last

    zero = jnp.zeros((channels, 128), jnp.float32)
    first, last = lax.fori_loop(0, slots, donate, (zero, zero), unroll=8)
    rim_out[0] = first
    rim_out[1] = last

    sends = []
    for n, m in enumerate((0, lon_count - 1)):
        copy = pltpu.make_async_remote_copy(
            src_ref=rim_out.at[n], dst_ref=rim_in.at[i], send_sem=rim_send.at[n],
            recv_sem=rim_recv.at[i], device_id=(1 - p, m, j), device_id_type=MESH,
        )
        copy.start()
        sends.append(copy)

    @pl.when(is_rim)
    def _():
        total = zero
        for m in range(lon_count):
            pltpu.make_async_remote_copy(
                src_ref=rim_out.at[0], dst_ref=rim_in.at[m], send_sem=rim_send.at[0],
                recv_sem=rim_recv.at[m], device_id=(1 - p, m, j), device_id_type=MESH,
            ).wait_recv()
            total = total + rim_in[m]
        out_ref[jnp.where(i == 0, 0, rows - 1)] = total

    for copy, there, _ in copies:
        pl.when(there)(copy.wait_send)
    for copy in sends:
        copy.wait_send()


def body(fields, offsets, fractions, send_count, send_owner, send_cell, send_target, send_frac):
    _, channels, rows, columns = fields.shape
    lon_count, lat_count = lax.axis_size("lon"), lax.axis_size("lat")
    slots = send_owner.shape[-1]
    groups = rows // PER
    hbm = pl.BlockSpec(memory_space=pltpu.HBM)
    vmem = pl.BlockSpec(memory_space=pltpu.VMEM)
    f32 = jnp.float32
    out = pl.pallas_call(
        functools.partial(kernel, lon_count, lat_count, rows, channels, slots),
        out_shape=jax.ShapeDtypeStruct((rows, channels, columns), f32),
        in_specs=[hbm, pl.BlockSpec(memory_space=pltpu.SMEM)] + [hbm] * 6,
        out_specs=vmem,
        scratch_shapes=[
            pltpu.SMEM((2, 1, rows // TILE), jnp.int32),
            pltpu.SMEM(send_owner.shape, jnp.int32),
            pltpu.SMEM(send_cell.shape, jnp.int32),
            pltpu.SMEM(send_target.shape, jnp.int32),
            pltpu.SMEM(send_frac.shape, f32),
            pltpu.VMEM((channels * rows, columns), f32),
            pltpu.VMEM((2, rows, columns), f32),
            pltpu.VMEM((LOW + rows + HIGH, channels, columns), f32),
            pltpu.VMEM((LOW, channels, columns), f32),
            pltpu.VMEM((HIGH, channels, columns), f32),
            pltpu.VMEM((groups, channels, columns), f32),
            pltpu.VMEM((groups, channels, columns), f32),
            pltpu.VMEM((groups + 3, channels, columns), f32),
            pltpu.VMEM((groups + 3, channels, columns), f32),
            pltpu.VMEM((LOW + rows + HIGH, channels, columns), f32),
            pltpu.VMEM((8, rows, columns), f32),
            pltpu.VMEM((2, channels, columns), f32),
            pltpu.VMEM((lon_count, channels, columns), f32),
            pltpu.SemaphoreType.DMA((7,)),
            pltpu.SemaphoreType.DMA((9,)),
            pltpu.SemaphoreType.DMA((9,)),
            pltpu.SemaphoreType.DMA((2,)),
            pltpu.SemaphoreType.DMA((lon_count,)),
        ],
        compiler_params=pltpu.CompilerParams(
            collective_id=0, has_side_effects=True, vmem_limit_bytes=60 * 1024 * 1024
        ),
    )(
        offsets.reshape(2, 1, rows // TILE), send_count, send_owner, send_cell, send_target, send_frac,
        fields.reshape(channels * rows, columns), fractions.reshape(2, rows, columns),
    )
    return out.transpose(1, 0, 2)[None]


def solution(mesh):
    placed = (
        P("panel", None, "lon", "lat"),
        P("panel", None, "lon", "lat"),
        P("panel", None, "lon", "lat"),
        P("panel", "lon", "lat"),
        P("panel", "lon", "lat", None),
        P("panel", "lon", "lat", None),
        P("panel", "lon", "lat", None),
        P("panel", "lon", "lat", None, None),
    )
    return jax.shard_map(
        body, mesh=mesh, in_specs=placed, out_specs=P("panel", None, "lon", "lat"), check_vma=False
    )
```

time: 28.6 us -> 21.9 us (0.77)
  Pallas kernels: 24.4 us -> 19.3 us
  local copies, waits for them, and re-layouts: 3.26 us -> 1.82 us
    pallas_call x1, Pallas kernels: 24.4 us -> 19.3 us  [body(): pl.pallas_call(functools.partial(kernel, lon_count, lat_count, rows, chan...]
    unnamed x14 -> x0, local copies, waits for them, and re-layouts: 2.44 us -> none
    broadcast_in_dim x1, local copies, waits for them, and re-layouts: 0.82 us -> 1.82 us  [body(): return out.transpose(1, 0, 2)[None]]
where the time goes in v2:
time: 21.9 us; the launch traced here: 21.7 us
  Pallas kernels  19.3 us (88%)
  local copies, waits for them, and re-layouts  1.82 us (8%)
  between operations  0.66 us (3%)
    pallas_call x1, Pallas kernels, body(): pl.pallas_call(functools.partial(kernel, lon_count, lat_count, rows, chan...  19.3 us
    broadcast_in_dim x1, local copies, waits for them, and re-layouts, body(): return out.transpose(1, 0, 2)[None]  1.82 us

profile of v2, /device:TPU:0, one launch (start us, length us, event | category | flops | bytes accessed | tf_op | source)
XLA Modules:
  0.0 21.7 jit_solution(10385498201765960303)
XLA Ops:
  0.7 19.3 %shard_map.82 = f32[32,24,128]{2,1,0:T(8,128)} custom-call(s32[2,1,4]{2,1,0:T(1,128)} %bitcast.11, s32[1,1,1]{2,1,0:T(1,128)S(6)} %copy.11.count, s32[1,1,1,64]{3,2,1,0:T(1,128)} %owner_hbm.1, s32[1,1,1,64]{3,2,1,0:T(1,128)} %cell_hbm.1, s32[1,1,1,64]{3,2,1,0:T(1,128)} %target_hbm.1, f32[1,1,1,2,64]{4,3,2,1,0:T(2,128)} %frac_hbm.1, f32[768,128]{1,0:T(8,128)} %bitcast.9, ...), custom_call_target="tpu_custom_call" | custom-call | tf_op jit(solution)/shard_map/pallas_call | solution.py:287
  19.9 1.8 %copy.10 = f32[1,24,32,128]{3,2,1,0:T(8,128)} copy(f32[1,24,32,128]{3,1,2,0:T(8,128)} %bitcast.8) | data formatting | bytes 786432 | tf_op jit(solution)/shard_map/broadcast_in_dim | solution.py:324

commit v3 on v2

v3 whole, which is shorter than its diff:
```python
import functools

import jax
import jax.numpy as jnp
from jax import lax
from jax.experimental import pallas as pl
from jax.experimental.pallas import tpu as pltpu
from jax.sharding import PartitionSpec as P

TILE = 8
LOW = 8
HIGH = 9
STRIP = 16
PER = 128 // STRIP
MESH = pl.DeviceIdType.MESH


def lagrange(x):
    return (
        -x * (x - 1.0) * (x - 2.0) * (1.0 / 6.0),
        (x + 1.0) * (x - 1.0) * (x - 2.0) * 0.5,
        -(x + 1.0) * x * (x - 2.0) * 0.5,
        (x + 1.0) * x * (x - 1.0) * (1.0 / 6.0),
    )


def kernel(
    lon_count, lat_count, rows, channels, slots,
    offsets_hbm, count, owner_hbm, cell_hbm, target_hbm, frac_hbm, x_hbm, tall_hbm, fractions_hbm, out_ref,
    offsets, owner, cell, target, frac, x_ref, frac_ref,
    ext, adv, land_lo, land_hi, land_one, pack_l, pack_r, from_r, from_l, halo, weights, rim_out, rim_in,
    in_sem, send_sem, recv_sem, rim_send, rim_recv,
):
    p = lax.axis_index("panel")
    i = lax.axis_index("lon")
    j = lax.axis_index("lat")
    groups = rows // PER
    blocks = channels // 8
    own = LOW
    has_prev, has_next = i > 0, i < lon_count - 1
    has_left, has_right = j > 0, j < lat_count - 1
    is_rim = jnp.logical_or(i == 0, i == lon_count - 1)

    around = [
        (-1, 0, has_prev), (1, 0, has_next), (0, -1, has_left), (0, 1, has_right),
        (-1, -1, has_prev & has_left), (1, -1, has_next & has_left),
        (-1, 1, has_prev & has_right), (1, 1, has_next & has_right),
    ]
    barrier = pltpu.get_barrier_semaphore()
    waits = jnp.int32(0)
    for di, dj, there in around:
        @pl.when(there)
        def _(di=di, dj=dj):
            pl.semaphore_signal(barrier, inc=1, device_id=(p, i + di, j + dj), device_id_type=MESH)
        waits = waits + there.astype(jnp.int32)

    @pl.when(is_rim)
    def _():
        def greet(m, carry):
            pl.semaphore_signal(barrier, inc=1, device_id=(1 - p, m, j), device_id_type=MESH)
            return carry
        lax.fori_loop(0, lon_count, greet, 0)

    @pl.when(jnp.logical_not(is_rim))
    def _():
        for m in (0, lon_count - 1):
            pl.semaphore_signal(barrier, inc=1, device_id=(1 - p, m, j), device_id_type=MESH)

    waits = waits + jnp.where(is_rim, lon_count, 2)

    loads = [
        pltpu.make_async_copy(src, dst, in_sem.at[n])
        for n, (src, dst) in enumerate([
            (tall_hbm, x_ref), (fractions_hbm, frac_ref), (offsets_hbm, offsets),
            (owner_hbm, owner), (cell_hbm, cell), (target_hbm, target), (frac_hbm, frac),
        ])
    ]
    for load in loads:
        load.start()

    def clear(ref, start, size):
        ref[pl.ds(start, size)] = jnp.zeros((size,) + ref.shape[1:], jnp.float32)

    @pl.when(jnp.logical_not(has_prev))
    def _():
        clear(land_lo, 0, blocks)
        clear(from_r, 0, 1)
        clear(from_l, 0, 1)

    @pl.when(jnp.logical_not(has_next))
    def _():
        clear(land_hi, 0, blocks)
        clear(land_one, 0, blocks)
        clear(from_r, 1 + groups, 2)
        clear(from_l, 1 + groups, 2)

    @pl.when(jnp.logical_not(has_right))
    def _():
        clear(from_r, 0, groups + 3)

    @pl.when(jnp.logical_not(has_left))
    def _():
        clear(from_l, 0, groups + 3)

    lane = lax.broadcasted_iota(jnp.int32, (8, 128), 1)
    strip = lane // STRIP

    def pack(g):
        for c in range(blocks):
            left = jnp.zeros((8, 128), jnp.float32)
            right = jnp.zeros((8, 128), jnp.float32)
            for m in range(PER):
                row = g * PER + m
                v = x_ref[pl.ds(c * 8 * rows + row, 8, stride=rows), :]
                ext[c, own + row] = v
                rolled = pltpu.roll(v, STRIP * m, 1) if m else v
                left = jnp.where(strip == m, rolled, left)
                right = jnp.where(strip == (m + PER - 1) % PER, rolled, right)
            pack_l[g, pl.ds(c * 8, 8), :] = left
            pack_r[g, pl.ds(c * 8, 8), :] = right

    copies = []

    def send(src, dst, side):
        di, dj, there = around[side]
        n = len(copies)
        copy = pltpu.make_async_remote_copy(
            src_ref=src, dst_ref=dst, send_sem=send_sem.at[n], recv_sem=recv_sem.at[n],
            device_id=(p, i + di, j + dj), device_id_type=MESH,
        )
        arrives = [t for a, b, t in around if (a, b) == (-di, -dj)][0]
        copies.append((copy, there, arrives))
        pl.when(there)(copy.start)

    def arrive(n):
        copy, _, arrives = copies[n]
        pl.when(arrives)(copy.wait_recv)

    pl.semaphore_wait(barrier, waits)
    for c in range(blocks):
        part = pl.ds(c * 8, 8)
        send(x_hbm.at[part, pl.ds(0, 8), :], land_hi.at[c], 0)
        send(x_hbm.at[part, pl.ds(rows - LOW, LOW), :], land_lo.at[c], 1)
    loads[0].wait()
    for g in range(groups):
        pack(g)
    send(pack_l, from_r.at[pl.ds(1, groups)], 2)
    send(pack_r, from_l.at[pl.ds(1, groups)], 3)
    send(pack_l.at[pl.ds(0, 2)], from_r.at[pl.ds(1 + groups, 2)], 4)
    send(pack_l.at[pl.ds(groups - 1, 1)], from_r.at[pl.ds(0, 1)], 5)
    send(pack_r.at[pl.ds(0, 2)], from_l.at[pl.ds(1 + groups, 2)], 6)
    send(pack_r.at[pl.ds(groups - 1, 1)], from_l.at[pl.ds(0, 1)], 7)
    send(ext.at[:, own + 8], land_one, 0)

    loads[1].wait()
    for g in range(groups):
        at = pl.ds(g * 8, 8)
        for axis in range(2):
            for n, w in enumerate(lagrange(frac_ref[axis, at, :])):
                weights[4 * axis + n, at, :] = w
    for load in loads[2:]:
        load.wait()

    def unpack(g, count):
        for c in range(blocks):
            at = pl.ds(c * 8, 8)
            for m in range(count):
                a, b = from_r[g, at, :], from_l[g, at, :]
                if m:
                    a = pltpu.roll(a, 128 - STRIP * m, 1)
                    b = pltpu.roll(b, 128 - STRIP * m, 1)
                halo[c, g * PER + m] = jnp.where(lane < 64, a, b)

    def tile(t, c):
        start = t * TILE + LOW - 1 + offsets[0, 0, t]
        shift = offsets[1, 0, t]
        inside, turn = [], []
        for b in range(4):
            k = shift + (b - 1)
            inside.append((lane >= k) & (lane < 128 + k))
            turn.append((256 - k) & 127)
        shifted = []
        for r in range(TILE):
            while len(shifted) < r + 4:
                main, edge = ext[c, start + len(shifted)], halo[c, start + len(shifted)]
                shifted.append(
                    [pltpu.roll(jnp.where(inside[b], main, edge), turn[b], 1) for b in range(4)]
                )
            row = t * TILE + r
            w = [jnp.broadcast_to(weights[n, pl.ds(row, 1), :], (8, 128)) for n in range(8)]
            total = None
            for a in range(4):
                inner = w[4] * shifted[r + a][0]
                for b in range(1, 4):
                    inner = inner + w[4 + b] * shifted[r + a][b]
                total = w[a] * inner if total is None else total + w[a] * inner
            adv[c, row] = total
            out_ref[pl.ds(c * 8 * rows + row, 8, stride=rows), :] = total

    live = count[0, 0, 0]

    def donate(c, k, carry):
        first, last = carry
        place = cell[0, 0, 0, k]
        row, col = place >> 7, place & 127
        to = target[0, 0, 0, k]
        a, b = frac[0, 0, 0, 0, k], frac[0, 0, 0, 1, k]
        to_first = owner[0, 0, 0, k] == 0
        mixed = (1.0 - a) * adv[c, row] + a * adv[c, row + 1]
        here = (256 + to - col) & 127
        beyond = (255 + to - col) & 127
        value = (1.0 - b) * pltpu.roll(mixed, here, 1) + b * pltpu.roll(mixed, beyond, 1)
        to = jnp.where(k < live, to, 128)
        first = jnp.where(lane == jnp.where(to_first, to, 128), value, first)
        last = jnp.where(lane == jnp.where(to_first, 128, to), value, last)
        return first, last

    tiles = rows // TILE
    lat, diagonal, one = 2 * blocks, 2 * blocks + 2, 2 * blocks + 6
    for n in (lat, lat + 1):
        arrive(n)
    for g in range(1, 1 + groups):
        unpack(g, PER)
    for c in range(blocks):
        for t in range(1, tiles - 2):
            tile(t, c)
    for n in range(diagonal, diagonal + 4):
        arrive(n)
    unpack(0, PER)
    unpack(1 + groups, PER)
    unpack(2 + groups, 1)
    zero = jnp.zeros((8, 128), jnp.float32)
    sends = []
    for c in range(blocks):
        arrive(2 * c)
        arrive(2 * c + 1)
        if c == 0:
            arrive(one)
        ext[c, pl.ds(0, LOW)] = jnp.swapaxes(land_lo[c], 0, 1)
        ext[c, pl.ds(own + rows, 8)] = jnp.swapaxes(land_hi[c], 0, 1)
        ext[c, own + rows + 8] = land_one[c]
        for t in [0] + list(range(max(1, tiles - 2), tiles)):
            tile(t, c)
        first, last = lax.fori_loop(0, slots, functools.partial(donate, c), (zero, zero), unroll=8)
        rim_out[0, c] = first
        rim_out[1, c] = last
        for n, m in enumerate((0, lon_count - 1)):
            copy = pltpu.make_async_remote_copy(
                src_ref=rim_out.at[n, c], dst_ref=rim_in.at[i, c], send_sem=rim_send.at[n, c],
                recv_sem=rim_recv.at[i, c], device_id=(1 - p, m, j), device_id_type=MESH,
            )
            copy.start()
            sends.append(copy)

    @pl.when(is_rim)
    def _():
        rim_row = jnp.where(i == 0, 0, rows - 1)
        for c in range(blocks):
            total = zero
            for m in range(lon_count):
                pltpu.make_async_remote_copy(
                    src_ref=rim_out.at[0, c], dst_ref=rim_in.at[m, c], send_sem=rim_send.at[0, c],
                    recv_sem=rim_recv.at[m, c], device_id=(1 - p, m, j), device_id_type=MESH,
                ).wait_recv()
                total = total + rim_in[m, c]
            out_ref[pl.ds(c * 8 * rows + rim_row, 8, stride=rows), :] = total

    for copy, there, _ in copies:
        pl.when(there)(copy.wait_send)
    for copy in sends:
        copy.wait_send()


def body(fields, offsets, fractions, send_count, send_owner, send_cell, send_target, send_frac):
    _, channels, rows, columns = fields.shape
    lon_count, lat_count = lax.axis_size("lon"), lax.axis_size("lat")
    slots = send_owner.shape[-1]
    groups = rows // PER
    hbm = pl.BlockSpec(memory_space=pltpu.HBM)
    smem = pl.BlockSpec(memory_space=pltpu.SMEM)
    f32 = jnp.float32
    blocks = channels // 8
    reach = LOW + rows + HIGH
    operands = (
        offsets.reshape(2, 1, rows // TILE), send_owner, send_cell, send_target, send_frac,
        fields.reshape(channels, rows, columns), fields.reshape(channels * rows, columns),
        fractions.reshape(2, rows, columns),
    )
    operands = [pltpu.with_memory_space_constraint(x, pltpu.HBM) for x in operands]
    operands.insert(1, send_count)
    out = pl.pallas_call(
        functools.partial(kernel, lon_count, lat_count, rows, channels, slots),
        out_shape=jax.ShapeDtypeStruct((channels * rows, columns), f32),
        in_specs=[hbm, smem] + [hbm] * 7,
        out_specs=pl.BlockSpec(memory_space=pltpu.VMEM),
        scratch_shapes=[
            pltpu.SMEM((2, 1, rows // TILE), jnp.int32),
            pltpu.SMEM(send_owner.shape, jnp.int32),
            pltpu.SMEM(send_cell.shape, jnp.int32),
            pltpu.SMEM(send_target.shape, jnp.int32),
            pltpu.SMEM(send_frac.shape, f32),
            pltpu.VMEM((channels * rows, columns), f32),
            pltpu.VMEM((2, rows, columns), f32),
            pltpu.VMEM((blocks, reach, 8, columns), f32),
            pltpu.VMEM((blocks, rows, 8, columns), f32),
            pltpu.VMEM((blocks, 8, LOW, columns), f32),
            pltpu.VMEM((blocks, 8, 8, columns), f32),
            pltpu.VMEM((blocks, 8, columns), f32),
            pltpu.VMEM((groups, channels, columns), f32),
            pltpu.VMEM((groups, channels, columns), f32),
            pltpu.VMEM((groups + 3, channels, columns), f32),
            pltpu.VMEM((groups + 3, channels, columns), f32),
            pltpu.VMEM((blocks, reach, 8, columns), f32),
            pltpu.VMEM((8, rows, columns), f32),
            pltpu.VMEM((2, blocks, 8, columns), f32),
            pltpu.VMEM((lon_count, blocks, 8, columns), f32),
            pltpu.SemaphoreType.DMA((7,)),
            pltpu.SemaphoreType.DMA((2 * blocks + 7,)),
            pltpu.SemaphoreType.DMA((2 * blocks + 7,)),
            pltpu.SemaphoreType.DMA((2, blocks)),
            pltpu.SemaphoreType.DMA((lon_count, blocks)),
        ],
        compiler_params=pltpu.CompilerParams(
            collective_id=0, has_side_effects=True, vmem_limit_bytes=24 * 1024 * 1024
        ),
    )(*operands)
    return out.reshape(fields.shape)


def solution(mesh):
    placed = (
        P("panel", None, "lon", "lat"),
        P("panel", None, "lon", "lat"),
        P("panel", None, "lon", "lat"),
        P("panel", "lon", "lat"),
        P("panel", "lon", "lat", None),
        P("panel", "lon", "lat", None),
        P("panel", "lon", "lat", None),
        P("panel", "lon", "lat", None, None),
    )
    return jax.shard_map(
        body, mesh=mesh, in_specs=placed, out_specs=P("panel", None, "lon", "lat"), check_vma=False
    )
```

time: 21.9 us -> 22.1 us (level)
  Pallas kernels: 19.3 us -> 20.5 us
  local copies, waits for them, and re-layouts: 1.82 us -> 0.75 us
    broadcast_in_dim x1 -> x0, local copies, waits for them, and re-layouts: 1.82 us -> none  [body(): return out.transpose(1, 0, 2)[None]]
    pallas_call x1, Pallas kernels: 19.3 us -> 20.5 us  [body(): pl.pallas_call(functools.partial(kernel, lon_count, lat_count, rows, chan...]
    unnamed x0 -> x1, local copies, waits for them, and re-layouts: none -> 0.75 us
where the time goes in v3:
time: 22.1 us; the launch traced here: 21.9 us
  Pallas kernels  20.5 us (93%)
  local copies, waits for them, and re-layouts  0.75 us (3%)
  between operations  0.66 us (3%)
    pallas_call x1, Pallas kernels, body(): pl.pallas_call(functools.partial(kernel, lon_count, lat_count, rows, chan...  20.5 us
    unnamed x1, local copies, waits for them, and re-layouts  0.75 us

profile of v3, /device:TPU:0, one launch (start us, length us, event | category | flops | bytes accessed | tf_op | source)
XLA Modules:
  0.0 21.9 jit_solution(14051991132638628659)
XLA Ops:
  0.7 20.5 %shard_map.82 = f32[768,128]{1,0:T(8,128)S(1)} custom-call(s32[2,1,4]{2,1,0:T(1,128)} %bitcast.11, s32[1,1,1]{2,1,0:T(1,128)S(6)} %copy.11.count, s32[1,1,1,64]{3,2,1,0:T(1,128)} %owner_hbm.1, s32[1,1,1,64]{3,2,1,0:T(1,128)} %cell_hbm.1, s32[1,1,1,64]{3,2,1,0:T(1,128)} %target_hbm.1, f32[1,1,1,2,64]{4,3,2,1,0:T(2,128)} %frac_hbm.1, f32[24,32,128]{2,1,0:T(8,128)} %bitcast.8, ...), custom_call_target="tpu_custom_call" | custom-call | tf_op jit(solution)/shard_map/pallas_call | solution.py:291
  21.1 0.7 %copy.12 = f32[1,24,32,128]{3,2,1,0:T(8,128)} copy(f32[1,24,32,128]{3,2,1,0:T(8,128)S(1)} %bitcast.7) | data formatting | bytes 786432

commit v4 on v3

--- a/solution.py
+++ b/solution.py
@@ -28,7 +28,7 @@
     lon_count, lat_count, rows, channels, slots,
     offsets_hbm, count, owner_hbm, cell_hbm, target_hbm, frac_hbm, x_hbm, tall_hbm, fractions_hbm, out_ref,
     offsets, owner, cell, target, frac, x_ref, frac_ref,
-    ext, adv, land_lo, land_hi, land_one, pack_l, pack_r, from_r, from_l, halo, weights, rim_out, rim_in,
+    ext, adv, land_lo, land_hi, land_one, pack_l, pack_r, from_r, from_l, halo, weights, slot_rows, rim_out, rim_in,
     in_sem, send_sem, recv_sem, rim_send, rim_recv,
 ):
     p = lax.axis_index("panel")
@@ -160,6 +160,24 @@
                 weights[4 * axis + n, at, :] = w
     for load in loads[2:]:
         load.wait()
+
+    live = count[0, 0, 0]
+    line = lax.broadcasted_iota(jnp.int32, (1, 128), 1)
+
+    def lay_out(k, carry):
+        col = cell[0, 0, 0, k] & 127
+        a, b = frac[0, 0, 0, 0, k], frac[0, 0, 0, 1, k]
+        to = jnp.where(k < live, target[0, 0, 0, k], 128)
+        to_first = owner[0, 0, 0, k] == 0
+        across = jnp.where(line == col, 1.0 - b, jnp.where(line == col + 1, b, 0.0))
+        at = pl.ds(k, 1)
+        slot_rows[0, at, :] = (1.0 - a) * across
+        slot_rows[1, at, :] = a * across
+        slot_rows[2, at, :] = jnp.where(line == jnp.where(to_first, to, 128), 1.0, 0.0)
+        slot_rows[3, at, :] = jnp.where(line == jnp.where(to_first, 128, to), 1.0, 0.0)
+        return carry
+
+    lax.fori_loop(0, slots, lay_out, 0, unroll=8)
 
     def unpack(g, count):
         for c in range(blocks):
@@ -197,23 +215,13 @@
             adv[c, row] = total
             out_ref[pl.ds(c * 8 * rows + row, 8, stride=rows), :] = total
 
-    live = count[0, 0, 0]
-
     def donate(c, k, carry):
         first, last = carry
-        place = cell[0, 0, 0, k]
-        row, col = place >> 7, place & 127
-        to = target[0, 0, 0, k]
-        a, b = frac[0, 0, 0, 0, k], frac[0, 0, 0, 1, k]
-        to_first = owner[0, 0, 0, k] == 0
-        mixed = (1.0 - a) * adv[c, row] + a * adv[c, row + 1]
-        here = (256 + to - col) & 127
-        beyond = (255 + to - col) & 127
-        value = (1.0 - b) * pltpu.roll(mixed, here, 1) + b * pltpu.roll(mixed, beyond, 1)
-        to = jnp.where(k < live, to, 128)
-        first = jnp.where(lane == jnp.where(to_first, to, 128), value, first)
-        last = jnp.where(lane == jnp.where(to_first, 128, to), value, last)
-        return first, last
+        row = cell[0, 0, 0, k] >> 7
+        at = pl.ds(k, 1)
+        mixed = slot_rows[0, at, :] * adv[c, row] + slot_rows[1, at, :] * adv[c, row + 1]
+        value = jnp.sum(mixed, axis=1, keepdims=True)
+        return first + slot_rows[2, at, :] * value, last + slot_rows[3, at, :] * value
 
     tiles = rows // TILE
     lat, diagonal, one = 2 * blocks, 2 * blocks + 2, 2 * blocks + 6
@@ -312,6 +320,7 @@
             pltpu.VMEM((groups + 3, channels, columns), f32),
             pltpu.VMEM((blocks, reach, 8, columns), f32),
             pltpu.VMEM((8, rows, columns), f32),
+            pltpu.VMEM((4, slots, columns), f32),
             pltpu.VMEM((2, blocks, 8, columns), f32),
             pltpu.VMEM((lon_count, blocks, 8, columns), f32),
             pltpu.SemaphoreType.DMA((7,)),

time: 22.1 us -> 21.9 us (level)
  no operation moved by 1% of the time
where the time goes in v4:
time: 21.9 us; the launch traced here: 21.7 us
  Pallas kernels  20.3 us (93%)
  local copies, waits for them, and re-layouts  0.75 us (3%)
  between operations  0.66 us (3%)
    pallas_call x1, Pallas kernels, body(): pl.pallas_call(functools.partial(kernel, lon_count, lat_count, rows, chan...  20.3 us
    unnamed x1, local copies, waits for them, and re-layouts  0.75 us

profile of v4, /device:TPU:0, one launch (start us, length us, event | category | flops | bytes accessed | tf_op | source)
XLA Modules:
  0.0 21.7 jit_solution(17114869560919407212)
XLA Ops:
  0.7 20.3 %shard_map.82 = f32[768,128]{1,0:T(8,128)S(1)} custom-call(s32[2,1,4]{2,1,0:T(1,128)} %bitcast.11, s32[1,1,1]{2,1,0:T(1,128)S(6)} %copy.11.count, s32[1,1,1,64]{3,2,1,0:T(1,128)} %owner_hbm.1, s32[1,1,1,64]{3,2,1,0:T(1,128)} %cell_hbm.1, s32[1,1,1,64]{3,2,1,0:T(1,128)} %target_hbm.1, f32[1,1,1,2,64]{4,3,2,1,0:T(2,128)} %frac_hbm.1, f32[24,32,128]{2,1,0:T(8,128)} %bitcast.8, ...), custom_call_target="tpu_custom_call" | custom-call | tf_op jit(solution)/shard_map/pallas_call | solution.py:299
  21.0 0.7 %copy.12 = f32[1,24,32,128]{3,2,1,0:T(8,128)} copy(f32[1,24,32,128]{3,2,1,0:T(8,128)S(1)} %bitcast.7) | data formatting | bytes 786432

commit v5 on v4

--- a/solution.py
+++ b/solution.py
@@ -28,7 +28,7 @@
     lon_count, lat_count, rows, channels, slots,
     offsets_hbm, count, owner_hbm, cell_hbm, target_hbm, frac_hbm, x_hbm, tall_hbm, fractions_hbm, out_ref,
     offsets, owner, cell, target, frac, x_ref, frac_ref,
-    ext, adv, land_lo, land_hi, land_one, pack_l, pack_r, from_r, from_l, halo, weights, slot_rows, rim_out, rim_in,
+    ext, adv, land_lo, land_hi, land_one, one_out, pack_l, pack_r, from_r, from_l, halo, weights, slot_rows, rim_out, rim_in,
     in_sem, send_sem, recv_sem, rim_send, rim_recv,
 ):
     p = lax.axis_index("panel")
@@ -137,11 +137,19 @@
         pl.when(arrives)(copy.wait_recv)
 
     pl.semaphore_wait(barrier, waits)
-    for c in range(blocks):
+
+    def send_tiles(c):
         part = pl.ds(c * 8, 8)
         send(x_hbm.at[part, pl.ds(0, 8), :], land_hi.at[c], 0)
         send(x_hbm.at[part, pl.ds(rows - LOW, LOW), :], land_lo.at[c], 1)
+
+    send_tiles(0)
     loads[0].wait()
+    for c in range(blocks):
+        one_out[c] = x_ref[pl.ds(c * 8 * rows + 8, 8, stride=rows), :]
+    send(one_out, land_one, 0)
+    for c in range(1, blocks - 1):
+        send_tiles(c)
     for g in range(groups):
         pack(g)
     send(pack_l, from_r.at[pl.ds(1, groups)], 2)
@@ -150,7 +158,7 @@
     send(pack_l.at[pl.ds(groups - 1, 1)], from_r.at[pl.ds(0, 1)], 5)
     send(pack_r.at[pl.ds(0, 2)], from_l.at[pl.ds(1 + groups, 2)], 6)
     send(pack_r.at[pl.ds(groups - 1, 1)], from_l.at[pl.ds(0, 1)], 7)
-    send(ext.at[:, own + 8], land_one, 0)
+    send_tiles(blocks - 1)
 
     loads[1].wait()
     for g in range(groups):
@@ -224,7 +232,8 @@
         return first + slot_rows[2, at, :] * value, last + slot_rows[3, at, :] * value
 
     tiles = rows // TILE
-    lat, diagonal, one = 2 * blocks, 2 * blocks + 2, 2 * blocks + 6
+    one, lat = 2, 2 * blocks + 1 - 2
+    diagonal, last_tiles = lat + 2, lat + 6
     for n in (lat, lat + 1):
         arrive(n)
     for g in range(1, 1 + groups):
@@ -240,8 +249,9 @@
     zero = jnp.zeros((8, 128), jnp.float32)
     sends = []
     for c in range(blocks):
-        arrive(2 * c)
-        arrive(2 * c + 1)
+        at = 0 if c == 0 else last_tiles if c == blocks - 1 else 2 * c + 1
+        arrive(at)
+        arrive(at + 1)
         if c == 0:
             arrive(one)
         ext[c, pl.ds(0, LOW)] = jnp.swapaxes(land_lo[c], 0, 1)
@@ -314,6 +324,7 @@
             pltpu.VMEM((blocks, 8, LOW, columns), f32),
             pltpu.VMEM((blocks, 8, 8, columns), f32),
             pltpu.VMEM((blocks, 8, columns), f32),
+            pltpu.VMEM((blocks, 8, columns), f32),
             pltpu.VMEM((groups, channels, columns), f32),
             pltpu.VMEM((groups, channels, columns), f32),
             pltpu.VMEM((groups + 3, channels, columns), f32),

time: 21.9 us -> 21.2 us (0.968)
  Pallas kernels: 20.3 us -> 19.6 us
    pallas_call x1, Pallas kernels: 20.3 us -> 19.6 us  [body(): pl.pallas_call(functools.partial(kernel, lon_count, lat_count, rows, chan...]
where the time goes in v5:
time: 21.2 us; the launch traced here: 21 us
  Pallas kernels  19.6 us (92%)
  local copies, waits for them, and re-layouts  0.75 us (4%)
  between operations  0.66 us (3%)
    pallas_call x1, Pallas kernels, body(): pl.pallas_call(functools.partial(kernel, lon_count, lat_count, rows, chan...  19.6 us
    unnamed x1, local copies, waits for them, and re-layouts  0.75 us

profile of v5, /device:TPU:0, one launch (start us, length us, event | category | flops | bytes accessed | tf_op | source)
XLA Modules:
  0.0 21.0 jit_solution(2483132655919138218)
XLA Ops:
  0.7 19.6 %shard_map.82 = f32[768,128]{1,0:T(8,128)S(1)} custom-call(s32[2,1,4]{2,1,0:T(1,128)} %bitcast.11, s32[1,1,1]{2,1,0:T(1,128)S(6)} %copy.11.count, s32[1,1,1,64]{3,2,1,0:T(1,128)} %owner_hbm.1, s32[1,1,1,64]{3,2,1,0:T(1,128)} %cell_hbm.1, s32[1,1,1,64]{3,2,1,0:T(1,128)} %target_hbm.1, f32[1,1,1,2,64]{4,3,2,1,0:T(2,128)} %frac_hbm.1, f32[24,32,128]{2,1,0:T(8,128)} %bitcast.8, ...), custom_call_target="tpu_custom_call" | custom-call | tf_op jit(solution)/shard_map/pallas_call | solution.py:309
  20.3 0.7 %copy.12 = f32[1,24,32,128]{3,2,1,0:T(8,128)} copy(f32[1,24,32,128]{3,2,1,0:T(8,128)S(1)} %bitcast.7) | data formatting | bytes 786432

commit v6 on v5

--- a/solution.py
+++ b/solution.py
@@ -105,67 +105,83 @@
     lane = lax.broadcasted_iota(jnp.int32, (8, 128), 1)
     strip = lane // STRIP
 
-    def pack(g):
-        for c in range(blocks):
-            left = jnp.zeros((8, 128), jnp.float32)
-            right = jnp.zeros((8, 128), jnp.float32)
-            for m in range(PER):
-                row = g * PER + m
-                v = x_ref[pl.ds(c * 8 * rows + row, 8, stride=rows), :]
-                ext[c, own + row] = v
-                rolled = pltpu.roll(v, STRIP * m, 1) if m else v
-                left = jnp.where(strip == m, rolled, left)
-                right = jnp.where(strip == (m + PER - 1) % PER, rolled, right)
-            pack_l[g, pl.ds(c * 8, 8), :] = left
-            pack_r[g, pl.ds(c * 8, 8), :] = right
+    def pack(n, carry):
+        g, c = n // blocks, n % blocks
+        left = jnp.zeros((8, 128), jnp.float32)
+        right = jnp.zeros((8, 128), jnp.float32)
+        for m in range(PER):
+            row = g * PER + m
+            v = x_ref[pl.ds(c * (8 * rows) + row, 8, stride=rows), :]
+            ext[c, own + row] = v
+            rolled = pltpu.roll(v, STRIP * m, 1) if m else v
+            left = jnp.where(strip == m, rolled, left)
+            right = jnp.where(strip == (m + PER - 1) % PER, rolled, right)
+        pack_l[g, c] = left
+        pack_r[g, c] = right
+        return carry
 
     copies = []
 
-    def send(src, dst, side):
+    def remote(src, dst, side, n):
         di, dj, there = around[side]
-        n = len(copies)
         copy = pltpu.make_async_remote_copy(
             src_ref=src, dst_ref=dst, send_sem=send_sem.at[n], recv_sem=recv_sem.at[n],
             device_id=(p, i + di, j + dj), device_id_type=MESH,
         )
         arrives = [t for a, b, t in around if (a, b) == (-di, -dj)][0]
-        copies.append((copy, there, arrives))
-        pl.when(there)(copy.start)
-
-    def arrive(n):
-        copy, _, arrives = copies[n]
-        pl.when(arrives)(copy.wait_recv)
+        return copy, there, arrives
+
+    def send(copy):
+        copies.append(copy)
+        pl.when(copy[1])(copy[0].start)
+
+    def arrive(copy):
+        pl.when(copy[2])(copy[0].wait_recv)
+
+    def edge_tiles(c):
+        part = pl.ds(pl.multiple_of(c * 8, 8), 8)
+        return (
+            remote(x_hbm.at[part, pl.ds(0, 8), :], land_hi.at[c], 0, 2 * c),
+            remote(x_hbm.at[part, pl.ds(rows - LOW, LOW), :], land_lo.at[c], 1, 2 * c + 1),
+        )
 
     pl.semaphore_wait(barrier, waits)
 
-    def send_tiles(c):
-        part = pl.ds(c * 8, 8)
-        send(x_hbm.at[part, pl.ds(0, 8), :], land_hi.at[c], 0)
-        send(x_hbm.at[part, pl.ds(rows - LOW, LOW), :], land_lo.at[c], 1)
-
-    send_tiles(0)
+    for copy in edge_tiles(0):
+        send(copy)
     loads[0].wait()
     for c in range(blocks):
         one_out[c] = x_ref[pl.ds(c * 8 * rows + 8, 8, stride=rows), :]
-    send(one_out, land_one, 0)
+    base = 2 * blocks
+    one = remote(one_out, land_one, 0, base)
+    send(one)
     for c in range(1, blocks - 1):
-        send_tiles(c)
-    for g in range(groups):
-        pack(g)
-    send(pack_l, from_r.at[pl.ds(1, groups)], 2)
-    send(pack_r, from_l.at[pl.ds(1, groups)], 3)
-    send(pack_l.at[pl.ds(0, 2)], from_r.at[pl.ds(1 + groups, 2)], 4)
-    send(pack_l.at[pl.ds(groups - 1, 1)], from_r.at[pl.ds(0, 1)], 5)
-    send(pack_r.at[pl.ds(0, 2)], from_l.at[pl.ds(1 + groups, 2)], 6)
-    send(pack_r.at[pl.ds(groups - 1, 1)], from_l.at[pl.ds(0, 1)], 7)
-    send_tiles(blocks - 1)
+        for copy in edge_tiles(c):
+            send(copy)
+    lax.fori_loop(0, groups * blocks, pack, 0)
+    strips = [
+        remote(pack_l, from_r.at[pl.ds(1, groups)], 2, base + 1),
+        remote(pack_r, from_l.at[pl.ds(1, groups)], 3, base + 2),
+        remote(pack_l.at[pl.ds(0, 2)], from_r.at[pl.ds(1 + groups, 2)], 4, base + 3),
+        remote(pack_l.at[pl.ds(groups - 1, 1)], from_r.at[pl.ds(0, 1)], 5, base + 4),
+        remote(pack_r.at[pl.ds(0, 2)], from_l.at[pl.ds(1 + groups, 2)], 6, base + 5),
+        remote(pack_r.at[pl.ds(groups - 1, 1)], from_l.at[pl.ds(0, 1)], 7, base + 6),
+    ]
+    for copy in strips:
+        send(copy)
+    for copy in edge_tiles(blocks - 1):
+        send(copy)
 
     loads[1].wait()
-    for g in range(groups):
-        at = pl.ds(g * 8, 8)
+
+    def weigh(g, carry):
+        at = pl.ds(pl.multiple_of(g * 8, 8), 8)
         for axis in range(2):
             for n, w in enumerate(lagrange(frac_ref[axis, at, :])):
                 weights[4 * axis + n, at, :] = w
+        return carry
+
+    lax.fori_loop(0, groups, weigh, 0)
     for load in loads[2:]:
         load.wait()
 
@@ -185,17 +201,15 @@
         slot_rows[3, at, :] = jnp.where(line == jnp.where(to_first, 128, to), 1.0, 0.0)
         return carry
 
-    lax.fori_loop(0, slots, lay_out, 0, unroll=8)
-
-    def unpack(g, count):
-        for c in range(blocks):
-            at = pl.ds(c * 8, 8)
-            for m in range(count):
-                a, b = from_r[g, at, :], from_l[g, at, :]
-                if m:
-                    a = pltpu.roll(a, 128 - STRIP * m, 1)
-                    b = pltpu.roll(b, 128 - STRIP * m, 1)
-                halo[c, g * PER + m] = jnp.where(lane < 64, a, b)
+    lax.fori_loop(0, slots, lay_out, 0, unroll=4)
+
+    def unpack(n, carry):
+        g, c = n // blocks, n % blocks
+        a, b = from_r[g, c], from_l[g, c]
+        for m in range(PER):
+            turned = [pltpu.roll(v, 128 - STRIP * m, 1) if m else v for v in (a, b)]
+            halo[c, g * PER + m] = jnp.where(lane < 64, turned[0], turned[1])
+        return carry
 
     def tile(t, c):
         start = t * TILE + LOW - 1 + offsets[0, 0, t]
@@ -213,7 +227,7 @@
                     [pltpu.roll(jnp.where(inside[b], main, edge), turn[b], 1) for b in range(4)]
                 )
             row = t * TILE + r
-            w = [jnp.broadcast_to(weights[n, pl.ds(row, 1), :], (8, 128)) for n in range(8)]
+            w = [weights[n, pl.ds(row, 1), :] for n in range(8)]
             total = None
             for a in range(4):
                 inner = w[4] * shifted[r + a][0]
@@ -221,7 +235,7 @@
                     inner = inner + w[4 + b] * shifted[r + a][b]
                 total = w[a] * inner if total is None else total + w[a] * inner
             adv[c, row] = total
-            out_ref[pl.ds(c * 8 * rows + row, 8, stride=rows), :] = total
+            out_ref[pl.ds(c * (8 * rows) + row, 8, stride=rows), :] = total
 
     def donate(c, k, carry):
         first, last = carry
@@ -232,48 +246,56 @@
         return first + slot_rows[2, at, :] * value, last + slot_rows[3, at, :] * value
 
     tiles = rows // TILE
-    one, lat = 2, 2 * blocks + 1 - 2
-    diagonal, last_tiles = lat + 2, lat + 6
-    for n in (lat, lat + 1):
-        arrive(n)
-    for g in range(1, 1 + groups):
-        unpack(g, PER)
-    for c in range(blocks):
-        for t in range(1, tiles - 2):
-            tile(t, c)
-    for n in range(diagonal, diagonal + 4):
-        arrive(n)
-    unpack(0, PER)
-    unpack(1 + groups, PER)
-    unpack(2 + groups, 1)
+    for copy in strips:
+        arrive(copy)
+    lax.fori_loop(0, (groups + 3) * blocks, unpack, 0)
+    first_inner, last_inner = 1, tiles - 2
+    inner = max(last_inner - first_inner, 0)
+    outer = tiles - inner
+
+    def inner_tile(n, carry):
+        tile(first_inner + n // blocks, n % blocks)
+        return carry
+
+    lax.fori_loop(0, inner * blocks, inner_tile, 0)
+    arrive(one)
     zero = jnp.zeros((8, 128), jnp.float32)
-    sends = []
-    for c in range(blocks):
-        at = 0 if c == 0 else last_tiles if c == blocks - 1 else 2 * c + 1
-        arrive(at)
-        arrive(at + 1)
-        if c == 0:
-            arrive(one)
+
+    def rim_copies(c):
+        return [
+            pltpu.make_async_remote_copy(
+                src_ref=rim_out.at[n, c], dst_ref=rim_in.at[i, c], send_sem=rim_send.at[n, c],
+                recv_sem=rim_recv.at[i, c], device_id=(1 - p, m, j), device_id_type=MESH,
+            )
+            for n, m in enumerate((0, lon_count - 1))
+        ]
+
+    def finish_block(c, carry):
+        for copy in edge_tiles(c):
+            arrive(copy)
         ext[c, pl.ds(0, LOW)] = jnp.swapaxes(land_lo[c], 0, 1)
         ext[c, pl.ds(own + rows, 8)] = jnp.swapaxes(land_hi[c], 0, 1)
         ext[c, own + rows + 8] = land_one[c]
-        for t in [0] + list(range(max(1, tiles - 2), tiles)):
-            tile(t, c)
+
+        def outer_tile(n, carry):
+            tile(jnp.where(n < first_inner, n, n + inner), c)
+            return carry
+
+        lax.fori_loop(0, outer, outer_tile, 0)
         first, last = lax.fori_loop(0, slots, functools.partial(donate, c), (zero, zero), unroll=8)
         rim_out[0, c] = first
         rim_out[1, c] = last
-        for n, m in enumerate((0, lon_count - 1)):
-            copy = pltpu.make_async_remote_copy(
-                src_ref=rim_out.at[n, c], dst_ref=rim_in.at[i, c], send_sem=rim_send.at[n, c],
-                recv_sem=rim_recv.at[i, c], device_id=(1 - p, m, j), device_id_type=MESH,
-            )
+        for copy in rim_copies(c):
             copy.start()
-            sends.append(copy)
+        return carry
+
+    lax.fori_loop(0, blocks, finish_block, 0)
 
     @pl.when(is_rim)
     def _():
         rim_row = jnp.where(i == 0, 0, rows - 1)
-        for c in range(blocks):
+
+        def collect(c, carry):
             total = zero
             for m in range(lon_count):
                 pltpu.make_async_remote_copy(
@@ -281,12 +303,16 @@
                     recv_sem=rim_recv.at[m, c], device_id=(1 - p, m, j), device_id_type=MESH,
                 ).wait_recv()
                 total = total + rim_in[m, c]
-            out_ref[pl.ds(c * 8 * rows + rim_row, 8, stride=rows), :] = total
+            out_ref[pl.ds(c * (8 * rows) + rim_row, 8, stride=rows), :] = total
+            return carry
+
+        lax.fori_loop(0, blocks, collect, 0)
 
     for copy, there, _ in copies:
         pl.when(there)(copy.wait_send)
-    for copy in sends:
-        copy.wait_send()
+    for c in range(blocks):
+        for copy in rim_copies(c):
+            copy.wait_send()
 
 
 def body(fields, offsets, fractions, send_count, send_owner, send_cell, send_target, send_frac):
@@ -325,11 +351,11 @@
             pltpu.VMEM((blocks, 8, 8, columns), f32),
             pltpu.VMEM((blocks, 8, columns), f32),
             pltpu.VMEM((blocks, 8, columns), f32),
-            pltpu.VMEM((groups, channels, columns), f32),
-            pltpu.VMEM((groups, channels, columns), f32),
-            pltpu.VMEM((groups + 3, channels, columns), f32),
-            pltpu.VMEM((groups + 3, channels, columns), f32),
-            pltpu.VMEM((blocks, reach, 8, columns), f32),
+            pltpu.VMEM((groups, blocks, 8, columns), f32),
+            pltpu.VMEM((groups, blocks, 8, columns), f32),
+            pltpu.VMEM((groups + 3, blocks, 8, columns), f32),
+            pltpu.VMEM((groups + 3, blocks, 8, columns), f32),
+            pltpu.VMEM((blocks, (groups + 3) * PER, 8, columns), f32),
             pltpu.VMEM((8, rows, columns), f32),
             pltpu.VMEM((4, slots, columns), f32),
             pltpu.VMEM((2, blocks, 8, columns), f32),

time: 21.2 us -> 23.8 us (1.12)
  Pallas kernels: 19.6 us -> 22.3 us
    pallas_call x1, Pallas kernels: 19.6 us -> 22.3 us  [body(): pl.pallas_call(functools.partial(kernel, lon_count, lat_count, rows, chan...]
where the time goes in v6:
time: 23.8 us; the launch traced here: 23.7 us
  Pallas kernels  22.3 us (94%)
  local copies, waits for them, and re-layouts  0.75 us (3%)
  between operations  0.66 us (3%)
    pallas_call x1, Pallas kernels, body(): pl.pallas_call(functools.partial(kernel, lon_count, lat_count, rows, chan...  22.3 us
    unnamed x1, local copies, waits for them, and re-layouts  0.75 us

profile of v6, /device:TPU:0, one launch (start us, length us, event | category | flops | bytes accessed | tf_op | source)
XLA Modules:
  0.0 23.7 jit_solution(9831950722694211032)
XLA Ops:
  0.7 22.3 %shard_map.82 = f32[768,128]{1,0:T(8,128)S(1)} custom-call(s32[2,1,4]{2,1,0:T(1,128)} %bitcast.11, s32[1,1,1]{2,1,0:T(1,128)S(6)} %copy.11.count, s32[1,1,1,64]{3,2,1,0:T(1,128)} %owner_hbm.1, s32[1,1,1,64]{3,2,1,0:T(1,128)} %cell_hbm.1, s32[1,1,1,64]{3,2,1,0:T(1,128)} %target_hbm.1, f32[1,1,1,2,64]{4,3,2,1,0:T(2,128)} %frac_hbm.1, f32[24,32,128]{2,1,0:T(8,128)} %bitcast.8, ...), custom_call_target="tpu_custom_call" | custom-call | tf_op jit(solution)/shard_map/pallas_call | solution.py:335
  22.9 0.7 %copy.12 = f32[1,24,32,128]{3,2,1,0:T(8,128)} copy(f32[1,24,32,128]{3,2,1,0:T(8,128)S(1)} %bitcast.7) | data formatting | bytes 786432

commit v7 on v5

--- a/solution.py
+++ b/solution.py
@@ -28,7 +28,7 @@
     lon_count, lat_count, rows, channels, slots,
     offsets_hbm, count, owner_hbm, cell_hbm, target_hbm, frac_hbm, x_hbm, tall_hbm, fractions_hbm, out_ref,
     offsets, owner, cell, target, frac, x_ref, frac_ref,
-    ext, adv, land_lo, land_hi, land_one, one_out, pack_l, pack_r, from_r, from_l, halo, weights, slot_rows, rim_out, rim_in,
+    ext, adv, land_lo, land_hi, land_one, one_out, pack_l, pack_r, strips, halo, weights, slot_rows, rim_out, rim_in,
     in_sem, send_sem, recv_sem, rim_send, rim_recv,
 ):
     p = lax.axis_index("panel")
@@ -37,6 +37,7 @@
     groups = rows // PER
     blocks = channels // 8
     own = LOW
+    from_r, from_l = strips.at[0], strips.at[1]
     has_prev, has_next = i > 0, i < lon_count - 1
     has_left, has_right = j > 0, j < lat_count - 1
     is_rim = jnp.logical_or(i == 0, i == lon_count - 1)
@@ -187,15 +188,21 @@
 
     lax.fori_loop(0, slots, lay_out, 0, unroll=8)
 
+    side = jnp.where(has_right, 0, 1)
+    kept = (lane < 64) == has_right
+
     def unpack(g, count):
         for c in range(blocks):
             at = pl.ds(c * 8, 8)
             for m in range(count):
-                a, b = from_r[g, at, :], from_l[g, at, :]
-                if m:
-                    a = pltpu.roll(a, 128 - STRIP * m, 1)
-                    b = pltpu.roll(b, 128 - STRIP * m, 1)
-                halo[c, g * PER + m] = jnp.where(lane < 64, a, b)
+                def turned(s):
+                    v = strips[s, g, at, :]
+                    return pltpu.roll(v, 128 - STRIP * m, 1) if m else v
+                if lat_count == 2:
+                    row = jnp.where(kept, turned(side), 0.0)
+                else:
+                    row = jnp.where(lane < 64, turned(0), turned(1))
+                halo[c, g * PER + m] = row
 
     def tile(t, c):
         start = t * TILE + LOW - 1 + offsets[0, 0, t]
@@ -259,7 +266,7 @@
         ext[c, own + rows + 8] = land_one[c]
         for t in [0] + list(range(max(1, tiles - 2), tiles)):
             tile(t, c)
-        first, last = lax.fori_loop(0, slots, functools.partial(donate, c), (zero, zero), unroll=8)
+        first, last = lax.fori_loop(0, slots, functools.partial(donate, c), (zero, zero), unroll=slots)
         rim_out[0, c] = first
         rim_out[1, c] = last
         for n, m in enumerate((0, lon_count - 1)):
@@ -327,8 +334,7 @@
             pltpu.VMEM((blocks, 8, columns), f32),
             pltpu.VMEM((groups, channels, columns), f32),
             pltpu.VMEM((groups, channels, columns), f32),
-            pltpu.VMEM((groups + 3, channels, columns), f32),
-            pltpu.VMEM((groups + 3, channels, columns), f32),
+            pltpu.VMEM((2, groups + 3, channels, columns), f32),
             pltpu.VMEM((blocks, reach, 8, columns), f32),
             pltpu.VMEM((8, rows, columns), f32),
             pltpu.VMEM((4, slots, columns), f32),

time: 21.2 us -> 19.4 us (0.915)
  Pallas kernels: 19.6 us -> 17.9 us
    pallas_call x1, Pallas kernels: 19.6 us -> 17.9 us  [body(): pl.pallas_call(functools.partial(kernel, lon_count, lat_count, rows, chan...]
where the time goes in v7:
time: 19.4 us; the launch traced here: 19.3 us
  Pallas kernels  17.9 us (92%)
  local copies, waits for them, and re-layouts  0.75 us (4%)
  between operations  0.66 us (3%)
    pallas_call x1, Pallas kernels, body(): pl.pallas_call(functools.partial(kernel, lon_count, lat_count, rows, chan...  17.9 us
    unnamed x1, local copies, waits for them, and re-layouts  0.75 us

profile of v7, /device:TPU:0, one launch (start us, length us, event | category | flops | bytes accessed | tf_op | source)
XLA Modules:
  0.0 19.3 jit_solution(18241653639703183704)
XLA Ops:
  0.7 17.9 %shard_map.82 = f32[768,128]{1,0:T(8,128)S(1)} custom-call(s32[2,1,4]{2,1,0:T(1,128)} %bitcast.11, s32[1,1,1]{2,1,0:T(1,128)S(6)} %copy.11.count, s32[1,1,1,64]{3,2,1,0:T(1,128)} %owner_hbm.1, s32[1,1,1,64]{3,2,1,0:T(1,128)} %cell_hbm.1, s32[1,1,1,64]{3,2,1,0:T(1,128)} %target_hbm.1, f32[1,1,1,2,64]{4,3,2,1,0:T(2,128)} %frac_hbm.1, f32[24,32,128]{2,1,0:T(8,128)} %bitcast.8, ...), custom_call_target="tpu_custom_call" | custom-call | tf_op jit(solution)/shard_map/pallas_call | solution.py:316
  18.5 0.7 %copy.12 = f32[1,24,32,128]{3,2,1,0:T(8,128)} copy(f32[1,24,32,128]{3,2,1,0:T(8,128)S(1)} %bitcast.7) | data formatting | bytes 786432

commit v8 on v7

--- a/solution.py
+++ b/solution.py
@@ -27,7 +27,7 @@
 def kernel(
     lon_count, lat_count, rows, channels, slots,
     offsets_hbm, count, owner_hbm, cell_hbm, target_hbm, frac_hbm, x_hbm, tall_hbm, fractions_hbm, out_ref,
-    offsets, owner, cell, target, frac, x_ref, frac_ref,
+    offsets, owner, cell, cell_line, target, frac, x_ref, frac_ref,
     ext, adv, land_lo, land_hi, land_one, one_out, pack_l, pack_r, strips, halo, weights, slot_rows, rim_out, rim_in,
     in_sem, send_sem, recv_sem, rim_send, rim_recv,
 ):
@@ -73,7 +73,7 @@
         pltpu.make_async_copy(src, dst, in_sem.at[n])
         for n, (src, dst) in enumerate([
             (tall_hbm, x_ref), (fractions_hbm, frac_ref), (offsets_hbm, offsets),
-            (owner_hbm, owner), (cell_hbm, cell), (target_hbm, target), (frac_hbm, frac),
+            (owner_hbm, owner), (cell_hbm, cell), (cell_hbm, cell_line), (target_hbm, target), (frac_hbm, frac),
         ])
     ]
     for load in loads:
@@ -171,22 +171,26 @@
         load.wait()
 
     live = count[0, 0, 0]
-    line = lax.broadcasted_iota(jnp.int32, (1, 128), 1)
-
-    def lay_out(k, carry):
-        col = cell[0, 0, 0, k] & 127
-        a, b = frac[0, 0, 0, 0, k], frac[0, 0, 0, 1, k]
-        to = jnp.where(k < live, target[0, 0, 0, k], 128)
-        to_first = owner[0, 0, 0, k] == 0
-        across = jnp.where(line == col, 1.0 - b, jnp.where(line == col + 1, b, 0.0))
-        at = pl.ds(k, 1)
-        slot_rows[0, at, :] = (1.0 - a) * across
-        slot_rows[1, at, :] = a * across
-        slot_rows[2, at, :] = jnp.where(line == jnp.where(to_first, to, 128), 1.0, 0.0)
-        slot_rows[3, at, :] = jnp.where(line == jnp.where(to_first, 128, to), 1.0, 0.0)
-        return carry
-
-    lax.fori_loop(0, slots, lay_out, 0, unroll=8)
+    f32 = jnp.float32
+    diagonal = lax.broadcasted_iota(jnp.int32, (slots, slots), 0) == lax.broadcasted_iota(
+        jnp.int32, (slots, slots), 1
+    )
+
+    def column(line):
+        line = jnp.broadcast_to(line.astype(f32), (slots, slots))
+        return jnp.sum(jnp.where(diagonal, line, 0.0), axis=1, keepdims=True)
+
+    is_live = lax.broadcasted_iota(jnp.int32, (1, slots), 1) < live
+    goal = jnp.where(is_live, target[0, 0], 128)
+    to_first = owner[0, 0] == 0
+    col = column(cell_line[0, 0] & 127)
+    a, b = column(frac[0, 0, 0, pl.ds(0, 1), :]), column(frac[0, 0, 0, pl.ds(1, 1), :])
+    place = lax.broadcasted_iota(jnp.int32, (slots, 128), 1).astype(f32)
+    across = jnp.where(place == col, 1.0 - b, jnp.where(place == col + 1.0, b, 0.0))
+    slot_rows[0] = (1.0 - a) * across
+    slot_rows[1] = a * across
+    slot_rows[2] = jnp.where(place == column(jnp.where(to_first, goal, 128)), 1.0, 0.0)
+    slot_rows[3] = jnp.where(place == column(jnp.where(to_first, 128, goal)), 1.0, 0.0)
 
     side = jnp.where(has_right, 0, 1)
     kept = (lane < 64) == has_right
@@ -240,7 +244,7 @@
 
     tiles = rows // TILE
     one, lat = 2, 2 * blocks + 1 - 2
-    diagonal, last_tiles = lat + 2, lat + 6
+    corners, last_tiles = lat + 2, lat + 6
     for n in (lat, lat + 1):
         arrive(n)
     for g in range(1, 1 + groups):
@@ -248,7 +252,7 @@
     for c in range(blocks):
         for t in range(1, tiles - 2):
             tile(t, c)
-    for n in range(diagonal, diagonal + 4):
+    for n in range(corners, corners + 4):
         arrive(n)
     unpack(0, PER)
     unpack(1 + groups, PER)
@@ -320,10 +324,11 @@
         out_specs=pl.BlockSpec(memory_space=pltpu.VMEM),
         scratch_shapes=[
             pltpu.SMEM((2, 1, rows // TILE), jnp.int32),
-            pltpu.SMEM(send_owner.shape, jnp.int32),
+            pltpu.VMEM(send_owner.shape, jnp.int32),
             pltpu.SMEM(send_cell.shape, jnp.int32),
-            pltpu.SMEM(send_target.shape, jnp.int32),
-            pltpu.SMEM(send_frac.shape, f32),
+            pltpu.VMEM(send_cell.shape, jnp.int32),
+            pltpu.VMEM(send_target.shape, jnp.int32),
+            pltpu.VMEM(send_frac.shape, f32),
             pltpu.VMEM((channels * rows, columns), f32),
             pltpu.VMEM((2, rows, columns), f32),
             pltpu.VMEM((blocks, reach, 8, columns), f32),
@@ -340,7 +345,7 @@
             pltpu.VMEM((4, slots, columns), f32),
             pltpu.VMEM((2, blocks, 8, columns), f32),
             pltpu.VMEM((lon_count, blocks, 8, columns), f32),
-            pltpu.SemaphoreType.DMA((7,)),
+            pltpu.SemaphoreType.DMA((8,)),
             pltpu.SemaphoreType.DMA((2 * blocks + 7,)),
             pltpu.SemaphoreType.DMA((2 * blocks + 7,)),
             pltpu.SemaphoreType.DMA((2, blocks)),

time: 19.4 us -> 19.4 us (level)
  no operation moved by 1% of the time
where the time goes in v8:
time: 19.4 us; the launch traced here: 19.3 us
  Pallas kernels  17.9 us (92%)
  local copies, waits for them, and re-layouts  0.75 us (4%)
  between operations  0.66 us (3%)
    pallas_call x1, Pallas kernels, body(): pl.pallas_call(functools.partial(kernel, lon_count, lat_count, rows, chan...  17.9 us
    unnamed x1, local copies, waits for them, and re-layouts  0.75 us

profile of v8, /device:TPU:0, one launch (start us, length us, event | category | flops | bytes accessed | tf_op | source)
XLA Modules:
  0.0 19.3 jit_solution(3407757401317226643)
XLA Ops:
  0.7 17.9 %shard_map.82 = f32[768,128]{1,0:T(8,128)S(1)} custom-call(s32[2,1,4]{2,1,0:T(1,128)} %bitcast.11, s32[1,1,1]{2,1,0:T(1,128)S(6)} %copy.11.count, s32[1,1,1,64]{3,2,1,0:T(1,128)} %owner_hbm.1, s32[1,1,1,64]{3,2,1,0:T(1,128)} %cell_hbm.1, s32[1,1,1,64]{3,2,1,0:T(1,128)} %target_hbm.1, f32[1,1,1,2,64]{4,3,2,1,0:T(2,128)} %frac_hbm.1, f32[24,32,128]{2,1,0:T(8,128)} %bitcast.8, ...), custom_call_target="tpu_custom_call" | custom-call | tf_op jit(solution)/shard_map/pallas_call | solution.py:320
  18.5 0.7 %copy.12 = f32[1,24,32,128]{3,2,1,0:T(8,128)} copy(f32[1,24,32,128]{3,2,1,0:T(8,128)S(1)} %bitcast.7) | data formatting | bytes 786432

commit v9 on v8

--- a/solution.py
+++ b/solution.py
@@ -276,28 +276,28 @@
         for n, m in enumerate((0, lon_count - 1)):
             copy = pltpu.make_async_remote_copy(
                 src_ref=rim_out.at[n, c], dst_ref=rim_in.at[i, c], send_sem=rim_send.at[n, c],
-                recv_sem=rim_recv.at[i, c], device_id=(1 - p, m, j), device_id_type=MESH,
+                recv_sem=rim_recv, device_id=(1 - p, m, j), device_id_type=MESH,
             )
             copy.start()
             sends.append(copy)
-
-    @pl.when(is_rim)
-    def _():
-        rim_row = jnp.where(i == 0, 0, rows - 1)
-        for c in range(blocks):
-            total = zero
-            for m in range(lon_count):
-                pltpu.make_async_remote_copy(
-                    src_ref=rim_out.at[0, c], dst_ref=rim_in.at[m, c], send_sem=rim_send.at[0, c],
-                    recv_sem=rim_recv.at[m, c], device_id=(1 - p, m, j), device_id_type=MESH,
-                ).wait_recv()
-                total = total + rim_in[m, c]
-            out_ref[pl.ds(c * 8 * rows + rim_row, 8, stride=rows), :] = total
 
     for copy, there, _ in copies:
         pl.when(there)(copy.wait_send)
     for copy in sends:
         copy.wait_send()
+
+    @pl.when(is_rim)
+    def _():
+        rim_row = jnp.where(i == 0, 0, rows - 1)
+        pltpu.make_async_remote_copy(
+            src_ref=rim_in, dst_ref=rim_in, send_sem=rim_send.at[0, 0], recv_sem=rim_recv,
+            device_id=(1 - p, i, j), device_id_type=MESH,
+        ).wait_recv()
+        for c in range(blocks):
+            total = rim_in[0, c]
+            for m in range(1, lon_count):
+                total = total + rim_in[m, c]
+            out_ref[pl.ds(c * 8 * rows + rim_row, 8, stride=rows), :] = total
 
 
 def body(fields, offsets, fractions, send_count, send_owner, send_cell, send_target, send_frac):
@@ -349,7 +349,7 @@
             pltpu.SemaphoreType.DMA((2 * blocks + 7,)),
             pltpu.SemaphoreType.DMA((2 * blocks + 7,)),
             pltpu.SemaphoreType.DMA((2, blocks)),
-            pltpu.SemaphoreType.DMA((lon_count, blocks)),
+            pltpu.SemaphoreType.DMA(()),
         ],
         compiler_params=pltpu.CompilerParams(
             collective_id=0, has_side_effects=True, vmem_limit_bytes=24 * 1024 * 1024

time: 19.4 us -> 19.2 us (0.990)
  Pallas kernels: 17.9 us -> 17.7 us
    pallas_call x1, Pallas kernels: 17.9 us -> 17.7 us  [body(): pl.pallas_call(functools.partial(kernel, lon_count, lat_count, rows, chan...]
where the time goes in v9:
time: 19.2 us; the launch traced here: 19.1 us
  Pallas kernels  17.7 us (92%)
  local copies, waits for them, and re-layouts  0.75 us (4%)
  between operations  0.66 us (3%)
    pallas_call x1, Pallas kernels, body(): pl.pallas_call(functools.partial(kernel, lon_count, lat_count, rows, chan...  17.7 us
    unnamed x1, local copies, waits for them, and re-layouts  0.75 us

profile of v9, /device:TPU:0, one launch (start us, length us, event | category | flops | bytes accessed | tf_op | source)
XLA Modules:
  0.0 19.1 jit_solution(18281041564300270053)
XLA Ops:
  0.7 17.7 %shard_map.82 = f32[768,128]{1,0:T(8,128)S(1)} custom-call(s32[2,1,4]{2,1,0:T(1,128)} %bitcast.11, s32[1,1,1]{2,1,0:T(1,128)S(6)} %copy.11.count, s32[1,1,1,64]{3,2,1,0:T(1,128)} %owner_hbm.1, s32[1,1,1,64]{3,2,1,0:T(1,128)} %cell_hbm.1, s32[1,1,1,64]{3,2,1,0:T(1,128)} %target_hbm.1, f32[1,1,1,2,64]{4,3,2,1,0:T(2,128)} %frac_hbm.1, f32[24,32,128]{2,1,0:T(8,128)} %bitcast.8, ...), custom_call_target="tpu_custom_call" | custom-call | tf_op jit(solution)/shard_map/pallas_call | solution.py:320
  18.3 0.7 %copy.12 = f32[1,24,32,128]{3,2,1,0:T(8,128)} copy(f32[1,24,32,128]{3,2,1,0:T(8,128)S(1)} %bitcast.7) | data formatting | bytes 786432
